TPU v7x, 32 devices: a whole 2x2x4 slice. The times are simulated.
32 devices in a mesh: groups: 2 (over x), col: 8 (over z, y), row: 2 (over core).
Axes of the slice: x: 2, y: 2, z: 4, core: 2. Of those that a mesh axis runs over, the one named last changes fastest.
Arguments:
- queries: bfloat16 [32, 8, 64, 1536], P(('groups', 'row'), 'col'), parts along dimension 0, may hold values from -300 to 300
- key_mant: bfloat16 [32, 8, 64, 1536], P(('groups', 'row'), 'col'), parts along dimension 0, may hold values from -8 to 8
- key_exp: int32 [32, 8, 2, 1536], P(('groups', 'row'), 'col'), parts along dimension 0, may hold values from -1 to 1
- value_mant: bfloat16 [32, 8, 64, 1536], P(('groups', 'row'), 'col'), parts along dimension 0, may hold values from -4 to 4
- value_exp: int32 [32, 8, 2, 1536], P(('groups', 'row'), 'col'), parts along dimension 0, may hold values from 0 to 2
- cycle_list: int32 [4, 8, 4], P(('groups', 'row'), 'col'), parts along dimension 0, may hold values from 0 to 17, as said below
- dilated_list: int32 [4, 8, 4], P(('groups', 'row'), 'col'), parts along dimension 0, may hold values from 0 to 13, as said below
Outputs:
- attended: bfloat16 [32, 8, 64, 1536], P(('groups', 'row'), 'col'), parts along dimension 0
There are 2 independent parts, one for each index of `groups`. A program takes and returns all parts, laid end to end along the dimension named above; each array names one. Nothing has to cross between parts.
Inputs may be any that keep to these rules, and one draw needn't show every extreme that they name: `cycle_list`: the 4 entries of a tile are distinct; none names a block outside the image, and every side of the cycle that lies inside the image is named at least once. `dilated_list`: the 4 entries of a tile are distinct.
All inputs are finite; a program needn't handle non-finite values.
Results may differ from a plain program's by a relative error of at most 0.0043.
Values may be sent and summed in bfloat16 or wider, within the bound.
A program may use at most 128 MiB of HBM per device.

v0:
```python
import jax
import jax.numpy as jnp
from jax import lax
from jax.sharding import PartitionSpec as P

HEADS = 12
HEAD_DIM = 128
DILATION_TILES = 8


def with_halo(cells, sides, width):
    for axis, dim in sides:
        count = lax.axis_size(axis)
        ends = count - 1
        head = lax.slice_in_dim(cells, 0, width, axis=dim)
        tail = lax.slice_in_dim(cells, cells.shape[dim] - width, cells.shape[dim], axis=dim)
        cells = jnp.concatenate(
            [
                lax.ppermute(tail, axis, [(i, (i + 1) % count) for i in range(ends)]),
                cells,
                lax.ppermute(head, axis, [((i + 1) % count, i) for i in range(ends)]),
            ],
            axis=dim,
        )
    return cells


def passed_along(block, axis, distance):
    devices = range(lax.axis_size(axis))
    route = [((i - distance) % len(devices), i) for i in devices]
    return lax.ppermute(block, axis, route)


def dequant(mantissa, exponent):
    tile_rows, tile_cols, block_length, feature_channel_width = mantissa.shape
    groups = exponent.shape[2]
    factor = jnp.exp2(exponent.astype(jnp.float32))[:, :, :, None, :]
    scaled = (
        mantissa.reshape(
            tile_rows, tile_cols, groups, block_length // groups, feature_channel_width
        ).astype(jnp.float32)
        * factor
    )
    return scaled.reshape(mantissa.shape).astype(jnp.bfloat16)


def attend_group(operands):
    query_part, key_part, value_part = operands
    scores = jnp.einsum(
        "qhd,khd->hqk", query_part, key_part, preferred_element_type=jnp.float32
    ) * HEAD_DIM ** (-0.5)
    row_max = jnp.max(scores, axis=-1, keepdims=True)
    weights = jnp.exp(scores - row_max)
    row_total = jnp.sum(weights, axis=-1)
    rounded = weights.astype(jnp.bfloat16)
    blended = jnp.einsum("hqk,khd->qhd", rounded, value_part, preferred_element_type=jnp.float32)
    return (blended / jnp.transpose(row_total)[:, :, None]).astype(jnp.bfloat16)


def per_device(queries, key_mant, key_exp, value_mant, value_exp, cycle_list, dilated_list):
    tile_blocks = queries.shape[0]
    block_length = queries.shape[2]
    feature_channel_width = queries.shape[3]
    distant_rows = tile_blocks // 4
    stacked = jnp.stack([dequant(key_mant, key_exp), dequant(value_mant, value_exp)])
    extended = with_halo(stacked, (("col", 2), ("row", 1)), 1)
    cycle_entry = cycle_list[0, 0]
    cycle_row = jnp.where(
        cycle_entry == 0,
        0,
        jnp.where(
            cycle_entry == 1,
            tile_blocks + 1,
            jnp.where(
                cycle_entry < tile_blocks + 2, cycle_entry - 1, cycle_entry - 1 - tile_blocks
            ),
        ),
    )
    cycle_col = jnp.where(cycle_entry < 2, 1, jnp.where(cycle_entry < tile_blocks + 2, 0, 2))
    extended_flat = extended.reshape(2, (tile_blocks + 2) * 3, block_length, feature_channel_width)
    cycle_blocks = jnp.take(extended_flat, cycle_row * 3 + cycle_col, axis=1)
    far_source = stacked[:, 0::4, 0]
    column_loop_length = lax.axis_size("col")
    step_spacing = column_loop_length // DILATION_TILES
    incoming_blocks = {}
    relayed = far_source
    for start_shift in range(1, DILATION_TILES):
        relayed = passed_along(relayed, "col", column_loop_length - step_spacing)
        incoming_blocks[start_shift] = relayed
    dilated_full_list = jnp.stack(
        [incoming_blocks[start_shift] for start_shift in range(1, DILATION_TILES)], axis=1
    ).reshape(2, (DILATION_TILES - 1) * distant_rows, block_length, feature_channel_width)
    dilated_blocks = jnp.take(dilated_full_list, dilated_list[0, 0], axis=1)
    own_blocks = stacked.reshape(2, tile_blocks, block_length, feature_channel_width)
    key_values = jnp.concatenate([own_blocks, cycle_blocks, dilated_blocks], axis=1)
    key_values = key_values.reshape(2, -1, HEADS // 2, 2, HEAD_DIM)
    token_count = tile_blocks * block_length
    query_groups = queries.reshape(token_count, HEADS // 2, 2, HEAD_DIM).transpose(1, 0, 2, 3)
    key_groups = key_values[0].transpose(1, 0, 2, 3)
    value_groups = key_values[1].transpose(1, 0, 2, 3)
    results = lax.map(attend_group, (query_groups, key_groups, value_groups))
    return results.transpose(1, 0, 2, 3).reshape(queries.shape)


def solution(mesh):
    in_specs = (
        P(("groups", "row"), "col", None, None),
        P(("groups", "row"), "col", None, None),
        P(("groups", "row"), "col", None, None),
        P(("groups", "row"), "col", None, None),
        P(("groups", "row"), "col", None, None),
        P(("groups", "row"), "col", None),
        P(("groups", "row"), "col", None),
    )
    out_specs = P(("groups", "row"), "col", None, None)
    return jax.shard_map(
        per_device, mesh=mesh, in_specs=in_specs, out_specs=out_specs, check_vma=False
    )
```

profile of v0, /device:TPU:0, one launch (start us, length us, event | category | flops | bytes accessed | tf_op | source)
XLA Modules:
  0.0 378.6 jit_solution(2773527997782003790)
XLA Ops:
  0.0 1.1 exponential_bitcast_fusion
  1.1 1.0 exponential_bitcast_fusion.1
  2.1 1.7 fusion.24
  4.1 3.1 fusion.29
  7.2 1.2 slice_bitcast_fusion
  8.4 6.1 %collective-permute-start.4 = (bf16[2,2,64,1536]{3,2,1,0:T(8,128)(2,1)S(1)}, bf16[2,2,64,1536]{3,2,1,0:T(8,128)(2,1)S(1)}, u32[]{:S(2)}, u32[]{:S(2)}) collective-permute-start(bf16[2,2,64,1536]{3,2,1,0:T(8,128)(2,1)S(1)} %slice_bitcast_fusion), channel_id=1, source_target_pairs={{2,0},{4,2},{6,4},{8,6},{10,8},{12,10},{14,12},{0,14},{3,1},{5,3},... | collective-permute-start | bytes 2359304 | tf_op jit(solution)/shard_map/ppermute | solution.py:31
  14.4 3.0 collective-permute-start
  17.4 1.3 collective-permute-start.1
  18.7 12.5 %collective-permute-done.4 = bf16[2,2,64,1536]{3,2,1,0:T(8,128)(2,1)S(1)} collective-permute-done((bf16[2,2,64,1536]{3,2,1,0:T(8,128)(2,1)S(1)}, bf16[2,2,64,1536]{3,2,1,0:T(8,128)(2,1)S(1)}, u32[]{:S(2)}, u32[]{:S(2)}) %collective-permute-start.4) | collective-permute-done | bytes 786464 | tf_op jit(solution)/shard_map/ppermute | solution.py:31
  32.1 69.1 %collective-permute-start.5 = (bf16[2,2,64,1536]{3,2,1,0:T(8,128)(2,1)S(1)}, bf16[2,2,64,1536]{3,2,1,0:T(8,128)(2,1)}, u32[]{:S(2)}, u32[]{:S(2)}) collective-permute-start(bf16[2,2,64,1536]{3,2,1,0:T(8,128)(2,1)S(1)} %collective-permute-done.4), channel_id=1, source_target_pairs={{2,0},{4,2},{6,4},{8,6},{10,8},{12,10},{14,12},{0,14},{3,1},{5,3},... | collective-permute-start | bytes 2359304 | tf_op jit(solution)/shard_map/ppermute | solution.py:31
  101.2 14.8 %collective-permute-done.5 = bf16[2,2,64,1536]{3,2,1,0:T(8,128)(2,1)} collective-permute-done((bf16[2,2,64,1536]{3,2,1,0:T(8,128)(2,1)S(1)}, bf16[2,2,64,1536]{3,2,1,0:T(8,128)(2,1)}, u32[]{:S(2)}, u32[]{:S(2)}) %collective-permute-start.5) | collective-permute-done | bytes 786464 | tf_op jit(solution)/shard_map/ppermute | solution.py:31
  116.0 67.4 %collective-permute-start.6 = (bf16[2,2,64,1536]{3,2,1,0:T(8,128)(2,1)}, bf16[2,2,64,1536]{3,2,1,0:T(8,128)(2,1)}, u32[]{:S(2)}, u32[]{:S(2)}) collective-permute-start(bf16[2,2,64,1536]{3,2,1,0:T(8,128)(2,1)} %collective-permute-done.5), channel_id=1, source_target_pairs={{2,0},{4,2},{6,4},{8,6},{10,8},{12,10},{14,12},{0,14},{3,1},{5,3},... | collective-permute-start | bytes 2359304 | tf_op jit(solution)/shard_map/ppermute | solution.py:31
  183.4 4.6 %reshape.222 = bf16[512,6,2,128]{3,2,1,0:T(2,128)(2,1)} reshape(bf16[8,1,64,1536]{3,2,1,0:T(8,128)(2,1)} %param.9) | data formatting | bytes 3145728 | tf_op jit(solution)/shard_map/reshape | solution.py:98
  188.0 11.6 %collective-permute-done.6 = bf16[2,2,64,1536]{3,2,1,0:T(8,128)(2,1)} collective-permute-done((bf16[2,2,64,1536]{3,2,1,0:T(8,128)(2,1)}, bf16[2,2,64,1536]{3,2,1,0:T(8,128)(2,1)}, u32[]{:S(2)}, u32[]{:S(2)}) %collective-permute-start.6) | collective-permute-done | bytes 786464 | tf_op jit(solution)/shard_map/ppermute | solution.py:31
  199.7 5.2 %collective-permute-start.7 = (bf16[2,2,64,1536]{3,2,1,0:T(8,128)(2,1)}, bf16[2,2,64,1536]{3,2,1,0:T(8,128)(2,1)S(1)}, u32[]{:S(2)}, u32[]{:S(2)}) collective-permute-start(bf16[2,2,64,1536]{3,2,1,0:T(8,128)(2,1)} %collective-permute-done.6), channel_id=1, source_target_pairs={{2,0},{4,2},{6,4},{8,6},{10,8},{12,10},{14,12},{0,14},{3,1},{5,3},... | collective-permute-start | bytes 2359304 | tf_op jit(solution)/shard_map/ppermute | solution.py:31
  204.8 1.2 bitcast_dynamic-update-slice_fusion.6
  206.0 1.2 bitcast_dynamic-update-slice_fusion.5
  207.2 12.9 %collective-permute-done.7 = bf16[2,2,64,1536]{3,2,1,0:T(8,128)(2,1)S(1)} collective-permute-done((bf16[2,2,64,1536]{3,2,1,0:T(8,128)(2,1)}, bf16[2,2,64,1536]{3,2,1,0:T(8,128)(2,1)S(1)}, u32[]{:S(2)}, u32[]{:S(2)}) %collective-permute-start.7) | collective-permute-done | bytes 786464 | tf_op jit(solution)/shard_map/ppermute | solution.py:31
  220.2 5.1 %collective-permute-start.8 = (bf16[2,2,64,1536]{3,2,1,0:T(8,128)(2,1)S(1)}, bf16[2,2,64,1536]{3,2,1,0:T(8,128)(2,1)S(1)}, u32[]{:S(2)}, u32[]{:S(2)}) collective-permute-start(bf16[2,2,64,1536]{3,2,1,0:T(8,128)(2,1)S(1)} %collective-permute-done.7), channel_id=1, source_target_pairs={{2,0},{4,2},{6,4},{8,6},{10,8},{12,10},{14,12},{0,14},{3,1},{5,3},... | collective-permute-start | bytes 2359304 | tf_op jit(solution)/shard_map/ppermute | solution.py:31
  225.2 1.6 pad_maximum_fusion.6
  226.9 1.4 collective-permute-start.2
  228.2 1.3 collective-permute-start.3
  229.5 1.2 bitcast_dynamic-update-slice_fusion.4
  230.7 8.6 %collective-permute-done.8 = bf16[2,2,64,1536]{3,2,1,0:T(8,128)(2,1)S(1)} collective-permute-done((bf16[2,2,64,1536]{3,2,1,0:T(8,128)(2,1)S(1)}, bf16[2,2,64,1536]{3,2,1,0:T(8,128)(2,1)S(1)}, u32[]{:S(2)}, u32[]{:S(2)}) %collective-permute-start.8) | collective-permute-done | bytes 786464 | tf_op jit(solution)/shard_map/ppermute | solution.py:31
  239.3 5.2 %collective-permute-start.9 = (bf16[2,2,64,1536]{3,2,1,0:T(8,128)(2,1)S(1)}, bf16[2,2,64,1536]{3,2,1,0:T(8,128)(2,1)}, u32[]{:S(2)}, u32[]{:S(2)}) collective-permute-start(bf16[2,2,64,1536]{3,2,1,0:T(8,128)(2,1)S(1)} %collective-permute-done.8), channel_id=1, source_target_pairs={{2,0},{4,2},{6,4},{8,6},{10,8},{12,10},{14,12},{0,14},{3,1},{5,3},... | collective-permute-start | bytes 2359304 | tf_op jit(solution)/shard_map/ppermute | solution.py:31
  244.6 13.0 %collective-permute-done.9 = bf16[2,2,64,1536]{3,2,1,0:T(8,128)(2,1)} collective-permute-done((bf16[2,2,64,1536]{3,2,1,0:T(8,128)(2,1)S(1)}, bf16[2,2,64,1536]{3,2,1,0:T(8,128)(2,1)}, u32[]{:S(2)}, u32[]{:S(2)}) %collective-permute-start.9) | collective-permute-done | bytes 786464 | tf_op jit(solution)/shard_map/ppermute | solution.py:31
  257.7 5.3 %collective-permute-start.10 = (bf16[2,2,64,1536]{3,2,1,0:T(8,128)(2,1)}, bf16[2,2,64,1536]{3,2,1,0:T(8,128)(2,1)}, u32[]{:S(2)}, u32[]{:S(2)}) collective-permute-start(bf16[2,2,64,1536]{3,2,1,0:T(8,128)(2,1)} %collective-permute-done.9), channel_id=1, source_target_pairs={{2,0},{4,2},{6,4},{8,6},{10,8},{12,10},{14,12},{0,14},{3,1},{5,3},... | collective-permute-start | bytes 2359304 | tf_op jit(solution)/shard_map/ppermute | solution.py:31
  262.9 8.6 %pad_maximum_fusion = bf16[2,10,3,64,1536]{4,3,2,1,0:T(8,128)(2,1)} fusion(bf16[2,1,3,64,1536]{4,3,2,1,0:T(8,128)(2,1)S(1)} %collective-permute-done.3, bf16[2,8,1,64,1536]{4,3,2,1,0:T(8,128)(2,1)} %collective-permute-done.1, bf16[1,8,1,64,1536]{4,3,2,1,0:T(8,128)(2,1)S(1)} %bitcast.108, bf16[1,8,1,64,1536]{4,3,2,1,0:T(8,128)(2,1)S(1)} %bitcast.111, ...), kind=kLoop, calls=%fused_computation.22 | loop fusion | flops 29491200 | bytes 23592960 | tf_op jit(solution)/shard_map/concatenate | solution.py:17
  271.5 6.2 %gather_fusion = bf16[4,2,64,1536]{3,2,1,0:T(8,128)(2,1)} fusion(bf16[2,30,64,1536]{3,2,1,0:T(8,128)(2,1)} %bitcast.112, s32[1024]{0:T(1024)S(1)} %pad_clamp_fusion.1), kind=kCustom, calls=%fused_computation | custom fusion | bytes 3145744 | tf_op jit(solution)/shard_map/jit(_take)/gather | solution.py:81
  277.7 2.1 bitcast_dynamic-update-slice_fusion.1
  279.8 2.1 bitcast_dynamic-update-slice_fusion
  281.8 5.6 %copy.13 = bf16[2,7,2,64,1536]{4,3,2,1,0:T(8,128)(2,1)} copy(bf16[2,7,2,64,1536]{4,3,2,0,1:T(8,128)(2,1)} %bitcast_dynamic-update-slice_fusion) | data formatting | bytes 11010048 | tf_op jit(solution)/shard_map/stack | solution.py:90
  287.4 4.5 %gather_fusion.1 = bf16[4,2,64,1536]{3,2,1,0:T(8,128)(2,1)} fusion(bf16[2,14,64,1536]{3,2,1,0:T(8,128)(2,1)} %bitcast.115, s32[1024]{0:T(1024)S(1)} %pad_clamp_fusion), kind=kCustom, calls=%fused_computation.1 | custom fusion | bytes 3145744 | tf_op jit(solution)/shard_map/jit(_take)/gather | solution.py:93
  291.9 1.7 select_bitcast_fusion
  294.7 2.2 fusion.31
  296.9 7.4 %squeeze.29 = bf16[1024,6,2,128]{3,2,1,0:T(2,128)(2,1)} reshape(bf16[1,16,64,1536]{3,2,1,0:T(8,128)(2,1)} %get-tuple-element.57) | data formatting | bytes 6291456 | tf_op jit(solution)/shard_map/squeeze | solution.py:100
  304.3 2.5 squeeze.30
  306.8 66.3 %while.10 = (s32[]{:T(128)}, bf16[6,512,2,128]{1,3,2,0:T(8,128)(2,1)}, bf16[6,1024,2,128]{3,2,0,1:T(2,128)(2,1)}, bf16[6,512,2,128]{3,2,0,1:T(2,128)(2,1)}, bf16[6,1024,2,128]{3,2,0,1:T(2,128)(2,1)}, /*index=5*/s32[]{:T(128)}) while((s32[]{:T(128)}, bf16[6,512,2,128]{1,3,2,0:T(8,128)(2,1)}, bf16[6,1024,2,128]{3,2,0,1:T(2,128)(2,1)}, ...), condition=%wide.region_3.4_spmd, body=%wide.region_0.3_spmd.sunk | while | flops 545519616 | bytes 34624104 | solution.py:101
  306.8 1.9 constant_dynamic-slice_fusion.5
  308.8 1.1 constant_dynamic-slice_fusion.6
  310.7 1.9 copy-done
  314.0 3.9 %fusion.41 = bf16[6,512,2,128]{1,3,2,0:T(8,128)(2,1)} fusion(bf16[6,512,2,128]{1,3,2,0:T(8,128)(2,1)} %get-tuple-element.106, s32[]{:T(128)} %get-tuple-element.105, f32[2,512,1024]{2,1,0:T(8,128)} %copy-done, f32[2,512]{1,0:T(2,128)S(1)} %get-tuple-element.97, bf16[1,1024,2,128]{1,3,2,0:T(8,128)(2,1)S(1)} %copy.40, f32[512,2]{0,1:T(2,128)S(1)} %bitcast.118), kind=kOutput, calls=%fused_computation.13.clone.1 | convolution fusion | flops 271843328 | bytes 4989440 | tf_op jit(solution)/shard_map/while/body/eval_jaxpr/hqk,khd->qhd/dot_general | solution.py:56
  317.9 1.9 constant_dynamic-slice_fusion.5
  319.8 1.1 constant_dynamic-slice_fusion.6
  321.8 1.9 copy-done
  325.1 3.9 %fusion.41 = bf16[6,512,2,128]{1,3,2,0:T(8,128)(2,1)} fusion(bf16[6,512,2,128]{1,3,2,0:T(8,128)(2,1)} %get-tuple-element.106, s32[]{:T(128)} %get-tuple-element.105, f32[2,512,1024]{2,1,0:T(8,128)} %copy-done, f32[2,512]{1,0:T(2,128)S(1)} %get-tuple-element.97, bf16[1,1024,2,128]{1,3,2,0:T(8,128)(2,1)S(1)} %copy.40, f32[512,2]{0,1:T(2,128)S(1)} %bitcast.118), kind=kOutput, calls=%fused_computation.13.clone.1 | convolution fusion | flops 271843328 | bytes 4989440 | tf_op jit(solution)/shard_map/while/body/eval_jaxpr/hqk,khd->qhd/dot_general | solution.py:56
  329.0 1.9 constant_dynamic-slice_fusion.5
  330.9 1.1 constant_dynamic-slice_fusion.6
  332.8 1.9 copy-done
  336.1 3.9 %fusion.41 = bf16[6,512,2,128]{1,3,2,0:T(8,128)(2,1)} fusion(bf16[6,512,2,128]{1,3,2,0:T(8,128)(2,1)} %get-tuple-element.106, s32[]{:T(128)} %get-tuple-element.105, f32[2,512,1024]{2,1,0:T(8,128)} %copy-done, f32[2,512]{1,0:T(2,128)S(1)} %get-tuple-element.97, bf16[1,1024,2,128]{1,3,2,0:T(8,128)(2,1)S(1)} %copy.40, f32[512,2]{0,1:T(2,128)S(1)} %bitcast.118), kind=kOutput, calls=%fused_computation.13.clone.1 | convolution fusion | flops 271843328 | bytes 4989440 | tf_op jit(solution)/shard_map/while/body/eval_jaxpr/hqk,khd->qhd/dot_general | solution.py:56
  340.0 1.9 constant_dynamic-slice_fusion.5
  341.9 1.1 constant_dynamic-slice_fusion.6
  343.9 1.9 copy-done
  347.2 3.9 %fusion.41 = bf16[6,512,2,128]{1,3,2,0:T(8,128)(2,1)} fusion(bf16[6,512,2,128]{1,3,2,0:T(8,128)(2,1)} %get-tuple-element.106, s32[]{:T(128)} %get-tuple-element.105, f32[2,512,1024]{2,1,0:T(8,128)} %copy-done, f32[2,512]{1,0:T(2,128)S(1)} %get-tuple-element.97, bf16[1,1024,2,128]{1,3,2,0:T(8,128)(2,1)S(1)} %copy.40, f32[512,2]{0,1:T(2,128)S(1)} %bitcast.118), kind=kOutput, calls=%fused_computation.13.clone.1 | convolution fusion | flops 271843328 | bytes 4989440 | tf_op jit(solution)/shard_map/while/body/eval_jaxpr/hqk,khd->qhd/dot_general | solution.py:56
  351.1 1.9 constant_dynamic-slice_fusion.5
  353.0 1.1 constant_dynamic-slice_fusion.6
  354.9 1.9 copy-done
  358.2 3.9 %fusion.41 = bf16[6,512,2,128]{1,3,2,0:T(8,128)(2,1)} fusion(bf16[6,512,2,128]{1,3,2,0:T(8,128)(2,1)} %get-tuple-element.106, s32[]{:T(128)} %get-tuple-element.105, f32[2,512,1024]{2,1,0:T(8,128)} %copy-done, f32[2,512]{1,0:T(2,128)S(1)} %get-tuple-element.97, bf16[1,1024,2,128]{1,3,2,0:T(8,128)(2,1)S(1)} %copy.40, f32[512,2]{0,1:T(2,128)S(1)} %bitcast.118), kind=kOutput, calls=%fused_computation.13.clone.1 | convolution fusion | flops 271843328 | bytes 4989440 | tf_op jit(solution)/shard_map/while/body/eval_jaxpr/hqk,khd->qhd/dot_general | solution.py:56
  362.1 1.9 constant_dynamic-slice_fusion.5
  364.0 1.1 constant_dynamic-slice_fusion.6
  366.0 1.9 copy-done
  369.3 3.9 %fusion.41 = bf16[6,512,2,128]{1,3,2,0:T(8,128)(2,1)} fusion(bf16[6,512,2,128]{1,3,2,0:T(8,128)(2,1)} %get-tuple-element.106, s32[]{:T(128)} %get-tuple-element.105, f32[2,512,1024]{2,1,0:T(8,128)} %copy-done, f32[2,512]{1,0:T(2,128)S(1)} %get-tuple-element.97, bf16[1,1024,2,128]{1,3,2,0:T(8,128)(2,1)S(1)} %copy.40, f32[512,2]{0,1:T(2,128)S(1)} %bitcast.118), kind=kOutput, calls=%fused_computation.13.clone.1 | convolution fusion | flops 271843328 | bytes 4989440 | tf_op jit(solution)/shard_map/while/body/eval_jaxpr/hqk,khd->qhd/dot_general | solution.py:56
  373.2 3.9 %copy.19 = bf16[512,6,2,128]{3,2,1,0:T(2,128)(2,1)S(1)} copy(bf16[512,6,2,128]{0,3,2,1:T(8,128)(2,1)} %bitcast.117) | data formatting | bytes 3145728 | tf_op jit(solution)/shard_map/transpose | solution.py:102
  377.1 1.5 reshape.223
  (54 shorter events, 15.3 us)
Async XLA Ops:
  0.0 3.8 copy-start.4
  4.1 97.1 %copy-start.7 = (s32[1,1,4]{2,1,0:T(1,128)S(1)}, s32[1,1,4]{2,1,0:T(1,128)}, u32[]{:S(2)}) copy-start(s32[1,1,4]{2,1,0:T(1,128)} %param.15) | copy-start | bytes 52
  7.2 180.8 %copy-start.6 = (s32[1,1,4]{2,1,0:T(1,128)S(1)}, s32[1,1,4]{2,1,0:T(1,128)}, u32[]{:S(2)}) copy-start(s32[1,1,4]{2,1,0:T(1,128)} %param.14) | copy-start | bytes 52
  8.4 22.9 %collective-permute-start.4 = (bf16[2,2,64,1536]{3,2,1,0:T(8,128)(2,1)S(1)}, bf16[2,2,64,1536]{3,2,1,0:T(8,128)(2,1)S(1)}, u32[]{:S(2)}, u32[]{:S(2)}) collective-permute-start(bf16[2,2,64,1536]{3,2,1,0:T(8,128)(2,1)S(1)} %slice_bitcast_fusion), channel_id=1, source_target_pairs={{2,0},{4,2},{6,4},{8,6},{10,8},{12,10},{14,12},{0,14},{3,1},{5,3},... | collective-permute-start | bytes 2359304 | tf_op jit(solution)/shard_map/ppermute | solution.py:31
  14.4 210.8 %collective-permute-start = (bf16[2,8,1,64,1536]{4,3,2,1,0:T(8,128)(2,1)}, bf16[2,8,1,64,1536]{4,3,2,1,0:T(8,128)(2,1)}, u32[]{:S(2)}, u32[]{:S(2)}) collective-permute-start(bf16[2,8,1,64,1536]{4,3,2,1,0:T(8,128)(2,1)} %get-tuple-element.59), channel_id=1, source_target_pairs={{0,2},{2,4},{4,6},{6,8},{8,10},{10,12},{12,14},{1,3},{3,5},{5,7},{... | collective-permute-start | bytes 9437192 | tf_op jit(solution)/shard_map/ppermute | solution.py:19
  17.4 207.8 %collective-permute-start.1 = (bf16[2,8,1,64,1536]{4,3,2,1,0:T(8,128)(2,1)}, bf16[2,8,1,64,1536]{4,3,2,1,0:T(8,128)(2,1)}, u32[]{:S(2)}, u32[]{:S(2)}) collective-permute-start(bf16[2,8,1,64,1536]{4,3,2,1,0:T(8,128)(2,1)} %get-tuple-element.59), channel_id=1, source_target_pairs={{2,0},{4,2},{6,4},{8,6},{10,8},{12,10},{14,12},{3,1},{5,3},{7,5},{... | collective-permute-start | bytes 9437192 | tf_op jit(solution)/shard_map/ppermute | solution.py:21
  31.2 0.9 copy-start.5
  32.1 83.8 %collective-permute-start.5 = (bf16[2,2,64,1536]{3,2,1,0:T(8,128)(2,1)S(1)}, bf16[2,2,64,1536]{3,2,1,0:T(8,128)(2,1)}, u32[]{:S(2)}, u32[]{:S(2)}) collective-permute-start(bf16[2,2,64,1536]{3,2,1,0:T(8,128)(2,1)S(1)} %collective-permute-done.4), channel_id=1, source_target_pairs={{2,0},{4,2},{6,4},{8,6},{10,8},{12,10},{14,12},{0,14},{3,1},{5,3},... | collective-permute-start | bytes 2359304 | tf_op jit(solution)/shard_map/ppermute | solution.py:31
  116.0 83.7 %collective-permute-start.6 = (bf16[2,2,64,1536]{3,2,1,0:T(8,128)(2,1)}, bf16[2,2,64,1536]{3,2,1,0:T(8,128)(2,1)}, u32[]{:S(2)}, u32[]{:S(2)}) collective-permute-start(bf16[2,2,64,1536]{3,2,1,0:T(8,128)(2,1)} %collective-permute-done.5), channel_id=1, source_target_pairs={{2,0},{4,2},{6,4},{8,6},{10,8},{12,10},{14,12},{0,14},{3,1},{5,3},... | collective-permute-start | bytes 2359304 | tf_op jit(solution)/shard_map/ppermute | solution.py:31
  199.7 20.5 %collective-permute-start.7 = (bf16[2,2,64,1536]{3,2,1,0:T(8,128)(2,1)}, bf16[2,2,64,1536]{3,2,1,0:T(8,128)(2,1)S(1)}, u32[]{:S(2)}, u32[]{:S(2)}) collective-permute-start(bf16[2,2,64,1536]{3,2,1,0:T(8,128)(2,1)} %collective-permute-done.6), channel_id=1, source_target_pairs={{2,0},{4,2},{6,4},{8,6},{10,8},{12,10},{14,12},{0,14},{3,1},{5,3},... | collective-permute-start | bytes 2359304 | tf_op jit(solution)/shard_map/ppermute | solution.py:31
  220.2 19.2 %collective-permute-start.8 = (bf16[2,2,64,1536]{3,2,1,0:T(8,128)(2,1)S(1)}, bf16[2,2,64,1536]{3,2,1,0:T(8,128)(2,1)S(1)}, u32[]{:S(2)}, u32[]{:S(2)}) collective-permute-start(bf16[2,2,64,1536]{3,2,1,0:T(8,128)(2,1)S(1)} %collective-permute-done.7), channel_id=1, source_target_pairs={{2,0},{4,2},{6,4},{8,6},{10,8},{12,10},{14,12},{0,14},{3,1},{5,3},... | collective-permute-start | bytes 2359304 | tf_op jit(solution)/shard_map/ppermute | solution.py:31
  226.9 36.1 %collective-permute-start.2 = (bf16[2,1,3,64,1536]{4,3,2,1,0:T(8,128)(2,1)S(1)}, bf16[2,1,3,64,1536]{4,3,2,1,0:T(8,128)(2,1)S(1)}, u32[]{:S(2)}, u32[]{:S(2)}) collective-permute-start(bf16[2,1,3,64,1536]{4,3,2,1,0:T(8,128)(2,1)S(1)} %get-tuple-element.54), channel_id=1, source_target_pairs={{0,1},{2,3},{4,5},{6,7},{8,9},{10,11},{12,13},{14,15},{16,17},{18,... | collective-permute-start | bytes 3538952 | tf_op jit(solution)/shard_map/ppermute | solution.py:19
  228.2 34.7 %collective-permute-start.3 = (bf16[2,1,3,64,1536]{4,3,2,1,0:T(8,128)(2,1)S(1)}, bf16[2,1,3,64,1536]{4,3,2,1,0:T(8,128)(2,1)S(1)}, u32[]{:S(2)}, u32[]{:S(2)}) collective-permute-start(bf16[2,1,3,64,1536]{4,3,2,1,0:T(8,128)(2,1)S(1)} %get-tuple-element.55), channel_id=1, source_target_pairs={{1,0},{3,2},{5,4},{7,6},{9,8},{11,10},{13,12},{15,14},{17,16},{19,... | collective-permute-start | bytes 3538952 | tf_op jit(solution)/shard_map/ppermute | solution.py:21
  239.3 18.3 %collective-permute-start.9 = (bf16[2,2,64,1536]{3,2,1,0:T(8,128)(2,1)S(1)}, bf16[2,2,64,1536]{3,2,1,0:T(8,128)(2,1)}, u32[]{:S(2)}, u32[]{:S(2)}) collective-permute-start(bf16[2,2,64,1536]{3,2,1,0:T(8,128)(2,1)S(1)} %collective-permute-done.8), channel_id=1, source_target_pairs={{2,0},{4,2},{6,4},{8,6},{10,8},{12,10},{14,12},{0,14},{3,1},{5,3},... | collective-permute-start | bytes 2359304 | tf_op jit(solution)/shard_map/ppermute | solution.py:31
  244.6 26.9 %copy-start.2 = (bf16[2,7,2,64,1536]{4,3,2,0,1:T(8,128)(2,1)}, bf16[2,7,2,64,1536]{4,3,2,0,1:T(8,128)(2,1)S(1)}, u32[]{:S(2)}) copy-start(bf16[2,7,2,64,1536]{4,3,2,0,1:T(8,128)(2,1)S(1)} %bitcast_dynamic-update-slice_fusion.2) | copy-start | bytes 16515076
  257.7 22.1 %collective-permute-start.10 = (bf16[2,2,64,1536]{3,2,1,0:T(8,128)(2,1)}, bf16[2,2,64,1536]{3,2,1,0:T(8,128)(2,1)}, u32[]{:S(2)}, u32[]{:S(2)}) collective-permute-start(bf16[2,2,64,1536]{3,2,1,0:T(8,128)(2,1)} %collective-permute-done.9), channel_id=1, source_target_pairs={{2,0},{4,2},{6,4},{8,6},{10,8},{12,10},{14,12},{0,14},{3,1},{5,3},... | collective-permute-start | bytes 2359304 | tf_op jit(solution)/shard_map/ppermute | solution.py:31
  287.4 6.3 %copy-start.1 = (bf16[2,8,64,1536]{3,2,1,0:T(8,128)(2,1)S(1)}, bf16[2,8,64,1536]{3,2,1,0:T(8,128)(2,1)}, u32[]{:S(2)}) copy-start(bf16[2,8,64,1536]{3,2,1,0:T(8,128)(2,1)} %get-tuple-element.58) | copy-start | bytes 9437188
  291.9 1.9 copy-start.3
  310.7 2.0 copy-start
  321.8 2.0 copy-start
  332.8 2.0 copy-start
  343.9 2.0 copy-start
  354.9 2.0 copy-start
  366.0 2.0 copy-start
where the time goes:
time: 380 us; the launch traced here: 379 us
  starting transfers between devices  170 us (45%)
  local copies, waits for them, and re-layouts  80.9 us (21%)
  waiting for transfers between devices  73.5 us (19%)
  matrix products  28.1 us (7%)
  other arithmetic  25.6 us (7%)
    ppermute x7, starting transfers between devices, passed_along(): return lax.ppermute(block, axis, route)  163 us
    ppermute x7, waiting for transfers between devices, passed_along(): return lax.ppermute(block, axis, route)  73.5 us
    dot_general x6, matrix products, attend_group(): jnp.einsum('hqk,khd->qhd', rounded, value_part, preferred_element_type=jn...  23.3 us
    dynamic_slice x18, local copies, waits for them, and re-layouts, per_device(): results = lax.map(attend_group, (query_groups, key_groups, value_groups))  20.8 us
    while x12, local copies, waits for them, and re-layouts  11.7 us
    concatenate x1, other arithmetic, with_halo(): jnp.concatenate([lax.ppermute(tail, axis, [(i, (i + 1) % count) for i in...  8.59 us
    another operation x2, local copies, waits for them, and re-layouts, per_device(): jnp.stack([incoming_blocks[start_shift] for start_shift in range(1, DILAT...  7.63 us
  transfers between devices with their start and end apart: 11, of which 6 were waited for; matrix products, arithmetic and copies ran while one was open for 7% of the time, Pallas kernels for 0%

commit v1 on v0

v1 whole, which is shorter than its diff:
```python
import functools
import math

import jax
import jax.numpy as jnp
from jax import lax
from jax.experimental import pallas as pl
from jax.experimental.pallas import tpu as pltpu
from jax.sharding import PartitionSpec as P

HEADS = 12
HEAD_DIM = 128
DILATION_TILES = 8
LINE = DILATION_TILES // 2
CHUNKS = 4
QUERY_TILE = 256
SLOTS = 3
MESH = pl.DeviceIdType.MESH


def request_tables(cycle_entry, dilated_entry, tile_blocks, member):
    is_left = (cycle_entry >= 2) & (cycle_entry < tile_blocks + 2)
    is_right = cycle_entry >= tile_blocks + 2

    def ranked(mask):
        before = jnp.arange(mask.shape[0])[:, None] > jnp.arange(mask.shape[0])[None, :]
        return jnp.sum((before & mask[None, :]).astype(jnp.int32), axis=1)

    def wanted(mask, rank, rows):
        slots = jnp.arange(SLOTS)[:, None]
        hit = mask[None, :] & (rank[None, :] == slots)
        return jnp.sum(jnp.where(hit, rows[None, :], 0), axis=1)

    left_rank, right_rank = ranked(is_left), ranked(is_right)
    left_rows = wanted(is_left, left_rank, cycle_entry - 2)
    right_rows = wanted(is_right, right_rank, cycle_entry - 2 - tile_blocks)
    cycle_slot = jnp.where(
        is_left, left_rank, jnp.where(is_right, SLOTS + right_rank, 2 * SLOTS)
    )
    distant_rows = tile_blocks // 4
    hop = dilated_entry // distant_rows + 1
    source = lax.rem(member + hop, DILATION_TILES)
    line_slot = (source // 2) * distant_rows + lax.rem(dilated_entry, distant_rows)
    crossing = lax.rem(hop, 2)
    asked = jnp.concatenate([line_slot * crossing, left_rows, right_rows]).astype(jnp.int32)
    asked = jnp.pad(asked[None, :], ((0, 7), (0, 128 - asked.shape[0])))
    places = jnp.concatenate([cycle_slot, line_slot * (1 - crossing), crossing])
    return asked, places.astype(jnp.int32)


def kernel(cols, blocks, places, q_ref, km_ref, ke_ref, vm_ref, ve_ref, asked, out_ref, *scratch):
    kv = scratch[0:CHUNKS]
    zbuf = scratch[CHUNKS : 2 * CHUNKS]
    pbuf = scratch[2 * CHUNKS : 3 * CHUNKS]
    cbuf = scratch[3 * CHUNKS : 4 * CHUNKS]
    psend = scratch[4 * CHUNKS : 5 * CHUNKS]
    csend = scratch[5 * CHUNKS : 6 * CHUNKS]
    (heard, heard_s, req_send, req_recv, req_local, z_send, z_recv, f_send, p_send, p_recv,
     c_send, c_recv, e_send, e_recv, v_send, v_recv) = scratch[6 * CHUNKS :]
    width = kv[0].shape[-1]
    block = kv[0].shape[-2]
    groups = ke_ref.shape[1]
    distant = blocks // 4
    spacing = cols // DILATION_TILES

    col = lax.axis_index("col")
    row = lax.axis_index("row")
    member, offset = col // spacing, lax.rem(col, spacing)
    gz, gy = member // 2, lax.rem(member, 2)

    def on_line(z):
        return {"col": (z * 2 + gy) * spacing + offset}

    partner = {"col": (gz * 2 + 1 - gy) * spacing + offset}
    left, right = {"col": col - 1}, {"col": col + 1}
    other = {"row": 1 - row}
    has_left, has_right = col > 0, col < cols - 1

    barrier = pltpu.get_barrier_semaphore()

    def greet(device):
        pl.semaphore_signal(barrier, inc=1, device_id=device, device_id_type=MESH)

    for z in range(LINE):
        pl.when(gz != z)(functools.partial(greet, on_line(z)))
    greet(partner)
    greet(other)
    pl.when(has_left)(functools.partial(greet, left))
    pl.when(has_right)(functools.partial(greet, right))

    def dequant(b):
        for which, (mant, expo) in enumerate(((km_ref, ke_ref), (vm_ref, ve_ref))):
            factor = lax.shift_left(jnp.int32(1), expo[b] + 8).astype(jnp.float32) * (2.0**-8)
            size = block // groups
            parts = [
                mant[b, g * size : (g + 1) * size, :].astype(jnp.float32) * factor[g : g + 1, :]
                for g in range(groups)
            ]
            full = jnp.concatenate(parts, axis=0).astype(jnp.bfloat16)
            for c in range(CHUNKS):
                kv[c][b, which] = full[:, c * width : (c + 1) * width]

    for r in range(distant):
        dequant(4 * r)
        for c in range(CHUNKS):
            zbuf[c][gz * distant + r] = kv[c][4 * r]

    pl.semaphore_wait(barrier, LINE + 1 + has_left.astype(jnp.int32) + has_right.astype(jnp.int32))

    def copy(src, dst, send, recv, device):
        return pltpu.make_async_remote_copy(
            src_ref=src, dst_ref=dst, send_sem=send, recv_sem=recv,
            device_id=device, device_id_type=MESH,
        )

    def ask(k, device):
        return copy(asked, heard.at[k], req_send.at[k], req_recv.at[k], device)

    ask(0, partner).start()
    pl.when(has_left)(lambda: ask(2, left).start())
    pl.when(has_right)(lambda: ask(1, right).start())

    def line_copy(c, source, z, sem):
        part = zbuf[c].at[pl.ds(source * distant, distant)]
        return copy(part, part, sem, z_recv.at[c, source], on_line(z))

    steps = (1, -1, 2, -2)

    def reaches(step):
        return (gz + step >= 0) & (gz + step < LINE)

    for c in range(CHUNKS):
        for k, step in enumerate(steps):
            pl.when(reaches(step))(
                lambda c=c, k=k, step=step: line_copy(c, gz, gz + step, z_send.at[c, k]).start()
            )

    for b in range(blocks):
        if b % 4:
            dequant(b)

    def vertical(c):
        src = kv[c].at[(1 - row) * (blocks - 1)]
        return copy(src, cbuf[c].at[2 * SLOTS], v_send.at[c], v_recv.at[c], other)

    for c in range(CHUNKS):
        vertical(c).start()

    def local(k):
        return pltpu.make_async_copy(heard.at[k], heard_s.at[k], req_local.at[k])

    def listen(k, device):
        ask(k, device).wait_recv()
        local(k).start()
        local(k).wait()

    listen(0, partner)
    pl.when(has_left)(lambda: listen(1, left))
    pl.when(has_right)(lambda: listen(2, right))

    def side_copy(c, side, device):
        base = SLOTS * (1 - side)
        return copy(
            csend[c].at[pl.ds(side * SLOTS, 2)], cbuf[c].at[pl.ds(base, 2)],
            c_send.at[c, side], c_recv.at[c, 1 - side], device,
        )

    def edge_copy(c, side, device):
        base = SLOTS * (1 - side)
        return copy(
            csend[c].at[side * SLOTS + 2], cbuf[c].at[base + 2],
            e_send.at[c, side], e_recv.at[c, 1 - side], device,
        )

    def send_sides(c):
        for side, exists, edge, device in (
            (0, has_left, col == 1, left), (1, has_right, col == cols - 2, right),
        ):
            @pl.when(exists)
            def _():
                at = 4 + (0 if side == 1 else SLOTS)
                k = 1 if side == 0 else 2
                for j in range(2):
                    csend[c][side * SLOTS + j] = kv[c][heard_s[k, 0, at + j]]
                side_copy(c, side, device).start()

            @pl.when(edge)
            def _():
                at = 4 + (0 if side == 1 else SLOTS)
                k = 1 if side == 0 else 2
                csend[c][side * SLOTS + 2] = kv[c][heard_s[k, 0, at + 2]]
                edge_copy(c, side, device).start()

    def forward(c):
        @pl.when(gz == 1)
        def _():
            line_copy(c, 3, 1, z_send.at[c, 0]).wait_recv()
            line_copy(c, 3, 0, f_send.at[c]).start()

        @pl.when(gz == 2)
        def _():
            line_copy(c, 0, 2, z_send.at[c, 0]).wait_recv()
            line_copy(c, 0, 3, f_send.at[c]).start()

    def partner_copy(c):
        return copy(psend[c], pbuf[c], p_send.at[c], p_recv.at[c], partner)

    def send_partner(c):
        for source in range(LINE):
            taken = ((gz == 1) & (source == 3)) | ((gz == 2) & (source == 0))
            pl.when((gz != source) & jnp.logical_not(taken))(
                lambda: line_copy(c, source, gz, z_send.at[c, 0]).wait_recv()
            )
        for i in range(4):
            psend[c][i] = zbuf[c][heard_s[0, 0, i]]
        partner_copy(c).start()

    def wait_inputs(c):
        partner_copy(c).wait_recv()
        vertical(c).wait_recv()
        pl.when(has_left)(lambda: side_copy(c, 1, left).wait_recv())
        pl.when(has_right)(lambda: side_copy(c, 0, right).wait_recv())
        pl.when(col == cols - 1)(lambda: edge_copy(c, 1, left).wait_recv())
        pl.when(col == 0)(lambda: edge_copy(c, 0, right).wait_recv())

    def attend(c):
        for i in range(4):
            kv[c][blocks + i] = cbuf[c][places[i]]
            kv[c][blocks + 4 + i] = jnp.where(
                places[8 + i] == 1, pbuf[c][i], zbuf[c][places[4 + i]]
            )
        factor = HEAD_DIM**-0.5 * math.log2(math.e)

        def tile(t, carry):
            rows = pl.ds(pl.multiple_of(t * QUERY_TILE, QUERY_TILE), QUERY_TILE)
            for h in range(width // HEAD_DIM):
                lanes = slice(h * HEAD_DIM, (h + 1) * HEAD_DIM)
                whole = slice(c * width + h * HEAD_DIM, c * width + (h + 1) * HEAD_DIM)
                keys = kv[c][:, 0, :, lanes].reshape(-1, HEAD_DIM)
                values = kv[c][:, 1, :, lanes].reshape(-1, HEAD_DIM)
                dots = lax.dot_general(
                    q_ref[rows, whole], keys, (((1,), (1,)), ((), ())),
                    preferred_element_type=jnp.float32,
                )
                top = jnp.max(dots, axis=-1, keepdims=True)
                weights = jnp.exp2((dots - top) * factor)
                total = jnp.sum(weights, axis=-1, keepdims=True)
                blended = jnp.dot(
                    weights.astype(jnp.bfloat16), values, preferred_element_type=jnp.float32
                )
                out_ref[rows, whole] = (blended / total).astype(jnp.bfloat16)
            return carry

        lax.fori_loop(0, q_ref.shape[0] // QUERY_TILE, tile, 0)

    for c in range(CHUNKS):
        send_sides(c)
    for c in range(CHUNKS):
        forward(c)
        send_partner(c)
        if c:
            wait_inputs(c - 1)
            attend(c - 1)
    wait_inputs(CHUNKS - 1)
    attend(CHUNKS - 1)

    ask(0, partner).wait_send()
    pl.when(has_left)(lambda: ask(2, left).wait_send())
    pl.when(has_right)(lambda: ask(1, right).wait_send())
    for c in range(CHUNKS):
        for k, step in enumerate(steps):
            pl.when(reaches(step))(
                lambda c=c, k=k, step=step: line_copy(c, gz, gz, z_send.at[c, k]).wait_send()
            )
        pl.when((gz == 1) | (gz == 2))(lambda: line_copy(c, 0, 0, f_send.at[c]).wait_send())
        partner_copy(c).wait_send()
        vertical(c).wait_send()
        pl.when(has_left)(lambda: side_copy(c, 0, left).wait_send())
        pl.when(has_right)(lambda: side_copy(c, 1, right).wait_send())
        pl.when(col == 1)(lambda: edge_copy(c, 0, left).wait_send())
        pl.when(col == cols - 2)(lambda: edge_copy(c, 1, right).wait_send())


def per_device(queries, key_mant, key_exp, value_mant, value_exp, cycle_list, dilated_list):
    blocks, _, block, features = queries.shape
    groups = key_exp.shape[2]
    cols = lax.axis_size("col")
    distant = blocks // 4
    width = features // CHUNKS
    member = lax.axis_index("col") // (cols // DILATION_TILES)
    asked, places = request_tables(cycle_list[0, 0], dilated_list[0, 0], blocks, member)
    vmem = pl.BlockSpec(memory_space=pltpu.VMEM)

    def buffers(slots):
        return [pltpu.VMEM((slots, 2, block, width), jnp.bfloat16)] * CHUNKS

    dma = pltpu.SemaphoreType.DMA
    tokens = blocks * block
    out = pl.pallas_call(
        functools.partial(kernel, cols, blocks),
        out_shape=jax.ShapeDtypeStruct((tokens, features), jnp.bfloat16),
        in_specs=[pl.BlockSpec(memory_space=pltpu.SMEM)] + [vmem] * 6,
        out_specs=vmem,
        scratch_shapes=[
            *buffers(blocks + 8), *buffers(LINE * distant), *buffers(4),
            *buffers(2 * SLOTS + 1), *buffers(4), *buffers(2 * SLOTS),
            pltpu.VMEM((3, 8, 128), jnp.int32), pltpu.SMEM((3, 8, 128), jnp.int32),
            dma((3,)), dma((3,)), dma((3,)),
            dma((CHUNKS, 4)), dma((CHUNKS, LINE)), dma((CHUNKS,)),
            dma((CHUNKS,)), dma((CHUNKS,)),
            dma((CHUNKS, 2)), dma((CHUNKS, 2)), dma((CHUNKS, 2)), dma((CHUNKS, 2)),
            dma((CHUNKS,)), dma((CHUNKS,)),
        ],
        compiler_params=pltpu.CompilerParams(
            collective_id=0, has_side_effects=True, vmem_limit_bytes=50 * 2**20
        ),
        cost_estimate=pl.CostEstimate(
            flops=8 * tokens * tokens * features, bytes_accessed=10 * tokens * features,
            transcendentals=2 * tokens * tokens * HEADS,
        ),
    )(
        places, queries.reshape(tokens, features),
        key_mant.reshape(blocks, block, features), key_exp.reshape(blocks, groups, features),
        value_mant.reshape(blocks, block, features), value_exp.reshape(blocks, groups, features),
        asked,
    )
    return out.reshape(queries.shape)


def solution(mesh):
    split = P(("groups", "row"), "col", None, None)
    lists = P(("groups", "row"), "col", None)
    return jax.shard_map(
        per_device, mesh=mesh, in_specs=(split,) * 5 + (lists,) * 2, out_specs=split,
        check_vma=False,
    )
```

time: 380 us -> 107 us (0.28)
  starting transfers between devices: 170 us -> 0 us
  Pallas kernels: 0 us -> 97.8 us
  local copies, waits for them, and re-layouts: 80.9 us -> 4.35 us
  waiting for transfers between devices: 73.5 us -> 0 us
  matrix products: 28.1 us -> 0 us
  other arithmetic: 25.6 us -> 3.2 us
    ppermute x11 -> x0, starting transfers between devices: 170 us -> none  [the longest x7 163 us: passed_along(): return lax.ppermute(block, axis, route)]
    pallas_call x0 -> x1, Pallas kernels: none -> 97.8 us  [per_device(): pl.pallas_call(functools.partial(kernel, cols, blocks), out_shape=jax.Sha...]
    ppermute x11 -> x0, waiting for transfers between devices: 73.5 us -> none  [the longest x7 73.5 us: passed_along(): return lax.ppermute(block, axis, route)]
    dot_general x12 -> x0, matrix products: 28.1 us -> none  [the longest x6 23.3 us: attend_group(): jnp.einsum('hqk,khd->qhd', rounded, value_part, preferred_element_type=jn...]
    dynamic_slice x18 -> x0, local copies, waits for them, and re-layouts: 20.8 us -> none  [per_device(): results = lax.map(attend_group, (query_groups, key_groups, value_groups))]
    while x12 -> x0, local copies, waits for them, and re-layouts: 11.7 us -> none
    squeeze x3 -> x0, local copies, waits for them, and re-layouts: 11.1 us -> none  [the longest x1 7.39 us: per_device(): value_groups = key_values[1].transpose(1, 0, 2, 3)]
    gather x2 -> x0, local copies, waits for them, and re-layouts: 10.7 us -> none  [the longest x1 6.15 us: per_device(): cycle_blocks = jnp.take(extended_flat, cycle_row * 3 + cycle_col, axis=1)]
  transfers between devices with their start and end apart: 11 -> 0, of which waited for: 6 -> 0; matrix products, arithmetic and copies ran while one was open for 7% -> 0% of each run, Pallas kernels for 0% -> 0%
where the time goes in v1:
time: 107 us; the launch traced here: 105 us
  Pallas kernels  97.8 us (91%)
  local copies, waits for them, and re-layouts  4.35 us (4%)
  other arithmetic  3.2 us (3%)
    pallas_call x1, Pallas kernels, per_device(): pl.pallas_call(functools.partial(kernel, cols, blocks), out_shape=jax.Sha...  97.8 us
    unnamed x7, local copies, waits for them, and re-layouts  4.35 us

profile of v1, /device:TPU:0, one launch (start us, length us, event | category | flops | bytes accessed | tf_op | source)
XLA Modules:
  0.0 105.4 jit_solution(4781753862185785037)
XLA Ops:
  0.0 0.7 fusion.7
  0.7 0.7 compare_bitcast_fusion
  1.3 0.1 convert_reduce_fusion
  1.5 0.1 convert_reduce_fusion.1
  1.6 0.7 subtract_multiply_fusion
  2.2 0.1 pad_add_fusion.places
  2.3 0.7 add_bitcast_fusion.2
  3.0 0.1 select_reduce_fusion
  3.1 0.1 add_bitcast_fusion
  3.2 0.0 copy-start
  3.2 1.4 %copy-done = bf16[8,1,64,1536]{3,2,1,0:T(8,128)(2,1)S(1)} copy-done((bf16[8,1,64,1536]{3,2,1,0:T(8,128)(2,1)S(1)}, bf16[8,1,64,1536]{3,2,1,0:T(8,128)(2,1)}, u32[]{:S(2)}) %copy-start) | copy-done | bytes 1572888
  4.6 0.0 copy-start.1
  4.6 0.9 copy-done.1
  5.5 0.0 copy-start.2
  5.5 0.9 copy-done.2
  6.4 97.8 %shard_map.73 = bf16[512,1536]{1,0:T(8,128)(2,1)S(1)} custom-call(s32[12]{0:T(128)S(1)} %pad_add_fusion.places, bf16[512,1536]{1,0:T(8,128)(2,1)S(1)} %bitcast.41, bf16[8,64,1536]{2,1,0:T(8,128)(2,1)} %bitcast.44, s32[8,2,1536]{2,1,0:T(2,128)S(1)} %bitcast.42, bf16[8,64,1536]{2,1,0:T(8,128)(2,1)} %bitcast.45, s32[8,2,1536]{2,1,0:T(2,128)S(1)} %bitcast.43, ...), custom_call_target="tpu_custom_call" | custom-call | flops 3221225472 | bytes 7864320 | tf_op jit(solution)/shard_map/pallas_call | solution.py:299
  104.3 1.1 %copy.11 = bf16[8,1,64,1536]{3,2,1,0:T(8,128)(2,1)} copy(bf16[8,1,64,1536]{3,2,1,0:T(8,128)(2,1)S(1)} %bitcast.40) | data formatting | bytes 3145728
  (1 shorter events, 0.0 us)
Async XLA Ops:
  3.2 1.4 %copy-start = (bf16[8,1,64,1536]{3,2,1,0:T(8,128)(2,1)S(1)}, bf16[8,1,64,1536]{3,2,1,0:T(8,128)(2,1)}, u32[]{:S(2)}) copy-start(bf16[8,1,64,1536]{3,2,1,0:T(8,128)(2,1)} %param.7) | copy-start | bytes 4718596
  4.6 0.9 copy-start.1
  5.5 0.9 copy-start.2

commit v2 on v1

--- a/solution.py
+++ b/solution.py
@@ -12,56 +12,69 @@
 HEAD_DIM = 128
 DILATION_TILES = 8
 LINE = DILATION_TILES // 2
-CHUNKS = 4
+CHUNK_HEADS = (1, 2, 2, 2, 2, 2, 1)
+CHUNKS = len(CHUNK_HEADS)
+STARTS = tuple(sum(CHUNK_HEADS[:c]) * HEAD_DIM for c in range(CHUNKS))
+WIDTHS = tuple(n * HEAD_DIM for n in CHUNK_HEADS)
+AHEAD = 3
 QUERY_TILE = 256
 SLOTS = 3
 MESH = pl.DeviceIdType.MESH
 
 
-def request_tables(cycle_entry, dilated_entry, tile_blocks, member):
-    is_left = (cycle_entry >= 2) & (cycle_entry < tile_blocks + 2)
-    is_right = cycle_entry >= tile_blocks + 2
-
-    def ranked(mask):
-        before = jnp.arange(mask.shape[0])[:, None] > jnp.arange(mask.shape[0])[None, :]
-        return jnp.sum((before & mask[None, :]).astype(jnp.int32), axis=1)
-
-    def wanted(mask, rank, rows):
-        slots = jnp.arange(SLOTS)[:, None]
-        hit = mask[None, :] & (rank[None, :] == slots)
-        return jnp.sum(jnp.where(hit, rows[None, :], 0), axis=1)
-
-    left_rank, right_rank = ranked(is_left), ranked(is_right)
-    left_rows = wanted(is_left, left_rank, cycle_entry - 2)
-    right_rows = wanted(is_right, right_rank, cycle_entry - 2 - tile_blocks)
-    cycle_slot = jnp.where(
-        is_left, left_rank, jnp.where(is_right, SLOTS + right_rank, 2 * SLOTS)
-    )
-    distant_rows = tile_blocks // 4
-    hop = dilated_entry // distant_rows + 1
+def side_entries(entries, low, high):
+    found, rank = [], jnp.int32(0)
+    for entry in entries:
+        hit = (entry >= low) & (entry < high)
+        found.append((hit, rank, entry - low))
+        rank = rank + hit.astype(jnp.int32)
+    return found
+
+
+def slot_rows(found, slots):
+    return [
+        sum(jnp.where(hit & (rank == slot), place, 0) for hit, rank, place in found)
+        for slot in range(slots)
+    ]
+
+
+def line_place(entry, member, distant):
+    hop = lax.div(entry, distant) + 1
     source = lax.rem(member + hop, DILATION_TILES)
-    line_slot = (source // 2) * distant_rows + lax.rem(dilated_entry, distant_rows)
-    crossing = lax.rem(hop, 2)
-    asked = jnp.concatenate([line_slot * crossing, left_rows, right_rows]).astype(jnp.int32)
-    asked = jnp.pad(asked[None, :], ((0, 7), (0, 128 - asked.shape[0])))
-    places = jnp.concatenate([cycle_slot, line_slot * (1 - crossing), crossing])
-    return asked, places.astype(jnp.int32)
-
-
-def kernel(cols, blocks, places, q_ref, km_ref, ke_ref, vm_ref, ve_ref, asked, out_ref, *scratch):
+    place = lax.div(source, 2) * distant + lax.rem(entry, distant)
+    return place, lax.rem(hop, 2) == 1
+
+
+def kernel(cols, blocks, cycle, dilated, q_hbm, km_hbm, ke_hbm, vm_hbm, ve_hbm, out_ref, *scratch):
     kv = scratch[0:CHUNKS]
     zbuf = scratch[CHUNKS : 2 * CHUNKS]
     pbuf = scratch[2 * CHUNKS : 3 * CHUNKS]
     cbuf = scratch[3 * CHUNKS : 4 * CHUNKS]
     psend = scratch[4 * CHUNKS : 5 * CHUNKS]
     csend = scratch[5 * CHUNKS : 6 * CHUNKS]
-    (heard, heard_s, req_send, req_recv, req_local, z_send, z_recv, f_send, p_send, p_recv,
+    (q_ref, km_ref, ke_ref, vm_ref, ve_ref, in_sem, asked, heard, heard_s, req_send, req_recv, req_local, z_send, z_recv, f_send, p_send, p_recv,
      c_send, c_recv, e_send, e_recv, v_send, v_recv) = scratch[6 * CHUNKS :]
-    width = kv[0].shape[-1]
     block = kv[0].shape[-2]
     groups = ke_ref.shape[1]
     distant = blocks // 4
     spacing = cols // DILATION_TILES
+
+    def fetch(src, dst, k):
+        return pltpu.make_async_copy(src, dst, in_sem.at[k])
+
+    pairs = ((km_hbm, km_ref), (vm_hbm, vm_ref))
+    exponents = [fetch(ke_hbm, ke_ref, 0), fetch(ve_hbm, ve_ref, 1)]
+    near = [
+        fetch(src.at[4 * r], dst.at[4 * r], 2 + 2 * r + k)
+        for r in range(distant) for k, (src, dst) in enumerate(pairs)
+    ]
+    far = [
+        fetch(src.at[pl.ds(4 * r + 1, 3)], dst.at[pl.ds(4 * r + 1, 3)], 2 + 2 * (distant + r) + k)
+        for r in range(distant) for k, (src, dst) in enumerate(pairs)
+    ]
+    queries = fetch(q_hbm, q_ref, 2 + 4 * distant)
+    for part in (*exponents, *near, *far, queries):
+        part.start()
 
     col = lax.axis_index("col")
     row = lax.axis_index("row")
@@ -98,8 +111,13 @@
             ]
             full = jnp.concatenate(parts, axis=0).astype(jnp.bfloat16)
             for c in range(CHUNKS):
-                kv[c][b, which] = full[:, c * width : (c + 1) * width]
-
+                kv[c][b, which] = full[:, STARTS[c] : STARTS[c] + WIDTHS[c]]
+
+    lane = lax.broadcasted_iota(jnp.int32, asked.shape, 1)
+    numbers = [cycle[i] for i in range(4)] + [dilated[i] for i in range(4)]
+    asked[...] = sum(jnp.where(lane == i, number, 0) for i, number in enumerate(numbers))
+    for part in (*exponents, *near):
+        part.wait()
     for r in range(distant):
         dequant(4 * r)
         for c in range(CHUNKS):
@@ -129,12 +147,16 @@
     def reaches(step):
         return (gz + step >= 0) & (gz + step < LINE)
 
-    for c in range(CHUNKS):
+    def send_line(c):
         for k, step in enumerate(steps):
             pl.when(reaches(step))(
-                lambda c=c, k=k, step=step: line_copy(c, gz, gz + step, z_send.at[c, k]).start()
+                lambda k=k, step=step: line_copy(c, gz, gz + step, z_send.at[c, k]).start()
             )
 
+    for c in range(AHEAD):
+        send_line(c)
+    for part in far:
+        part.wait()
     for b in range(blocks):
         if b % 4:
             dequant(b)
@@ -142,9 +164,6 @@
     def vertical(c):
         src = kv[c].at[(1 - row) * (blocks - 1)]
         return copy(src, cbuf[c].at[2 * SLOTS], v_send.at[c], v_recv.at[c], other)
-
-    for c in range(CHUNKS):
-        vertical(c).start()
 
     def local(k):
         return pltpu.make_async_copy(heard.at[k], heard_s.at[k], req_local.at[k])
@@ -172,24 +191,25 @@
             e_send.at[c, side], e_recv.at[c, 1 - side], device,
         )
 
+    sides = ((0, has_left, col == 1, left), (1, has_right, col == cols - 2, right))
+
     def send_sides(c):
-        for side, exists, edge, device in (
-            (0, has_left, col == 1, left), (1, has_right, col == cols - 2, right),
-        ):
+        vertical(c).start()
+        for side, exists, edge, device in sides:
+            low = 2 + blocks * (1 - side)
+
             @pl.when(exists)
             def _():
-                at = 4 + (0 if side == 1 else SLOTS)
-                k = 1 if side == 0 else 2
+                entries = [heard_s[1 + side, 0, i] for i in range(4)]
+                rows = slot_rows(side_entries(entries, low, low + blocks), SLOTS)
                 for j in range(2):
-                    csend[c][side * SLOTS + j] = kv[c][heard_s[k, 0, at + j]]
+                    csend[c][side * SLOTS + j] = kv[c][rows[j]]
                 side_copy(c, side, device).start()
 
-            @pl.when(edge)
-            def _():
-                at = 4 + (0 if side == 1 else SLOTS)
-                k = 1 if side == 0 else 2
-                csend[c][side * SLOTS + 2] = kv[c][heard_s[k, 0, at + 2]]
-                edge_copy(c, side, device).start()
+                @pl.when(edge)
+                def _():
+                    csend[c][side * SLOTS + 2] = kv[c][rows[2]]
+                    edge_copy(c, side, device).start()
 
     def forward(c):
         @pl.when(gz == 1)
@@ -212,7 +232,8 @@
                 lambda: line_copy(c, source, gz, z_send.at[c, 0]).wait_recv()
             )
         for i in range(4):
-            psend[c][i] = zbuf[c][heard_s[0, 0, i]]
+            place, _ = line_place(heard_s[0, 0, 4 + i], gz * 2 + 1 - gy, distant)
+            psend[c][i] = zbuf[c][place]
         partner_copy(c).start()
 
     def wait_inputs(c):
@@ -223,19 +244,26 @@
         pl.when(col == cols - 1)(lambda: edge_copy(c, 1, left).wait_recv())
         pl.when(col == 0)(lambda: edge_copy(c, 0, right).wait_recv())
 
+    entries = [cycle[i] for i in range(4)]
+    lefts = side_entries(entries, 2, 2 + blocks)
+    rights = side_entries(entries, 2 + blocks, 2 + 2 * blocks)
+    cycle_places = [
+        jnp.where(a[0], a[1], jnp.where(b[0], SLOTS + b[1], 2 * SLOTS))
+        for a, b in zip(lefts, rights)
+    ]
+
     def attend(c):
         for i in range(4):
-            kv[c][blocks + i] = cbuf[c][places[i]]
-            kv[c][blocks + 4 + i] = jnp.where(
-                places[8 + i] == 1, pbuf[c][i], zbuf[c][places[4 + i]]
-            )
+            kv[c][blocks + i] = cbuf[c][cycle_places[i]]
+            place, crossing = line_place(dilated[i], member, distant)
+            kv[c][blocks + 4 + i] = jnp.where(crossing, pbuf[c][i], zbuf[c][place])
         factor = HEAD_DIM**-0.5 * math.log2(math.e)
 
         def tile(t, carry):
             rows = pl.ds(pl.multiple_of(t * QUERY_TILE, QUERY_TILE), QUERY_TILE)
-            for h in range(width // HEAD_DIM):
+            for h in range(CHUNK_HEADS[c]):
                 lanes = slice(h * HEAD_DIM, (h + 1) * HEAD_DIM)
-                whole = slice(c * width + h * HEAD_DIM, c * width + (h + 1) * HEAD_DIM)
+                whole = slice(STARTS[c] + h * HEAD_DIM, STARTS[c] + (h + 1) * HEAD_DIM)
                 keys = kv[c][:, 0, :, lanes].reshape(-1, HEAD_DIM)
                 values = kv[c][:, 1, :, lanes].reshape(-1, HEAD_DIM)
                 dots = lax.dot_general(
@@ -253,11 +281,15 @@
 
         lax.fori_loop(0, q_ref.shape[0] // QUERY_TILE, tile, 0)
 
-    for c in range(CHUNKS):
+    for c in range(AHEAD):
         send_sides(c)
+    queries.wait()
     for c in range(CHUNKS):
         forward(c)
         send_partner(c)
+        if c + AHEAD < CHUNKS:
+            send_line(c + AHEAD)
+            send_sides(c + AHEAD)
         if c:
             wait_inputs(c - 1)
             attend(c - 1)
@@ -286,24 +318,33 @@
     groups = key_exp.shape[2]
     cols = lax.axis_size("col")
     distant = blocks // 4
-    width = features // CHUNKS
-    member = lax.axis_index("col") // (cols // DILATION_TILES)
-    asked, places = request_tables(cycle_list[0, 0], dilated_list[0, 0], blocks, member)
-    vmem = pl.BlockSpec(memory_space=pltpu.VMEM)
+    vmem = pltpu.VMEM
+    smem = pl.BlockSpec(memory_space=pltpu.SMEM)
+    anywhere = pl.BlockSpec(memory_space=pl.ANY)
 
     def buffers(slots):
-        return [pltpu.VMEM((slots, 2, block, width), jnp.bfloat16)] * CHUNKS
+        return [vmem((slots, 2, block, width), jnp.bfloat16) for width in WIDTHS]
 
     dma = pltpu.SemaphoreType.DMA
     tokens = blocks * block
     out = pl.pallas_call(
         functools.partial(kernel, cols, blocks),
         out_shape=jax.ShapeDtypeStruct((tokens, features), jnp.bfloat16),
-        in_specs=[pl.BlockSpec(memory_space=pltpu.SMEM)] + [vmem] * 6,
-        out_specs=vmem,
+        in_specs=[smem] * 2 + [anywhere] * 5,
+        out_specs=pl.BlockSpec(memory_space=vmem),
         scratch_shapes=[
             *buffers(blocks + 8), *buffers(LINE * distant), *buffers(4),
             *buffers(2 * SLOTS + 1), *buffers(4), *buffers(2 * SLOTS),
+            vmem((tokens, features), jnp.bfloat16),
+            *[
+                part
+                for _ in range(2)
+                for part in (
+                    vmem((blocks, block, features), jnp.bfloat16),
+                    vmem((blocks, groups, features), jnp.int32),
+                )
+            ],
+            dma((3 + 4 * distant,)), vmem((8, 128), jnp.int32),
             pltpu.VMEM((3, 8, 128), jnp.int32), pltpu.SMEM((3, 8, 128), jnp.int32),
             dma((3,)), dma((3,)), dma((3,)),
             dma((CHUNKS, 4)), dma((CHUNKS, LINE)), dma((CHUNKS,)),
@@ -312,17 +353,16 @@
             dma((CHUNKS,)), dma((CHUNKS,)),
         ],
         compiler_params=pltpu.CompilerParams(
-            collective_id=0, has_side_effects=True, vmem_limit_bytes=50 * 2**20
+            collective_id=0, has_side_effects=True, vmem_limit_bytes=60 * 2**20
         ),
         cost_estimate=pl.CostEstimate(
             flops=8 * tokens * tokens * features, bytes_accessed=10 * tokens * features,
             transcendentals=2 * tokens * tokens * HEADS,
         ),
     )(
-        places, queries.reshape(tokens, features),
+        cycle_list.reshape(-1), dilated_list.reshape(-1), queries.reshape(tokens, features),
         key_mant.reshape(blocks, block, features), key_exp.reshape(blocks, groups, features),
         value_mant.reshape(blocks, block, features), value_exp.reshape(blocks, groups, features),
-        asked,
     )
     return out.reshape(queries.shape)
 

time: 107 us -> 91.1 us (0.85); the launches traced: 105 us -> 91 us
  Pallas kernels: 97.8 us -> 88.3 us
  other arithmetic: 3.2 us -> 0 us
  local copies, waits for them, and re-layouts: 4.35 us -> 2.65 us
    pallas_call x1, Pallas kernels: 97.8 us -> 88.3 us  [per_device(): pl.pallas_call(functools.partial(kernel, cols, blocks), out_shape=jax.Sha...]
    unnamed x7 -> x1, local copies, waits for them, and re-layouts: 4.35 us -> 2.65 us
    mul x2 -> x0, other arithmetic: 1.34 us -> none  [the longest x1 0.68 us: request_tables(): line_slot * crossing]
where the time goes in v2:
time: 91.1 us; the launch traced here: 91 us
  Pallas kernels  88.3 us (97%)
  local copies, waits for them, and re-layouts  2.65 us (3%)
    pallas_call x1, Pallas kernels, per_device(): pl.pallas_call(functools.partial(kernel, cols, blocks), out_shape=jax.Sha...  88.3 us
    unnamed x1, local copies, waits for them, and re-layouts  2.65 us

profile of v2, /device:TPU:0, one launch (start us, length us, event | category | flops | bytes accessed | tf_op | source)
XLA Modules:
  0.0 91.0 jit_solution(12026115286294509147)
XLA Ops:
  0.0 88.3 %shard_map.73 = bf16[512,1536]{1,0:T(8,128)(2,1)} custom-call(s32[4]{0:T(128)} %bitcast.16, s32[4]{0:T(128)} %bitcast.17, bf16[512,1536]{1,0:T(8,128)(2,1)} %bitcast.11, bf16[8,64,1536]{2,1,0:T(8,128)(2,1)} %bitcast.12, s32[8,2,1536]{2,1,0:T(2,128)} %bitcast.14, bf16[8,64,1536]{2,1,0:T(8,128)(2,1)} %bitcast.13, s32[8,2,1536]{2,1,0:T(2,128)} %bitcast.15), custom_call_target="tpu_custom_call" | custom-call | flops 3221225472 | bytes 7864320 | tf_op jit(solution)/shard_map/pallas_call | solution.py:330
  88.3 2.7 %copy.10 = bf16[8,1,64,1536]{3,2,1,0:T(8,128)(2,1)} copy(bf16[8,1,64,1536]{3,2,1,0:T(8,128)(2,1)} %bitcast.10) | data formatting | bytes 3145728

commit v3 on v2

--- a/solution.py
+++ b/solution.py
@@ -17,6 +17,7 @@
 STARTS = tuple(sum(CHUNK_HEADS[:c]) * HEAD_DIM for c in range(CHUNKS))
 WIDTHS = tuple(n * HEAD_DIM for n in CHUNK_HEADS)
 AHEAD = 3
+DIRECT_CHUNKS = 2
 QUERY_TILE = 256
 SLOTS = 3
 MESH = pl.DeviceIdType.MESH
@@ -45,6 +46,10 @@
     return place, lax.rem(hop, 2) == 1
 
 
+def merges(cols, c):
+    return cols == DILATION_TILES and c >= DIRECT_CHUNKS
+
+
 def kernel(cols, blocks, cycle, dilated, q_hbm, km_hbm, ke_hbm, vm_hbm, ve_hbm, out_ref, *scratch):
     kv = scratch[0:CHUNKS]
     zbuf = scratch[CHUNKS : 2 * CHUNKS]
@@ -52,12 +57,16 @@
     cbuf = scratch[3 * CHUNKS : 4 * CHUNKS]
     psend = scratch[4 * CHUNKS : 5 * CHUNKS]
     csend = scratch[5 * CHUNKS : 6 * CHUNKS]
+    dsend = scratch[6 * CHUNKS : 7 * CHUNKS]
+    dbuf = scratch[7 * CHUNKS : 8 * CHUNKS]
     (q_ref, km_ref, ke_ref, vm_ref, ve_ref, in_sem, asked, heard, heard_s, req_send, req_recv, req_local, z_send, z_recv, f_send, p_send, p_recv,
-     c_send, c_recv, e_send, e_recv, v_send, v_recv) = scratch[6 * CHUNKS :]
+     c_send, c_recv, e_send, e_recv, v_send, v_recv, d_send, d_recv) = scratch[8 * CHUNKS :]
     block = kv[0].shape[-2]
     groups = ke_ref.shape[1]
     distant = blocks // 4
     spacing = cols // DILATION_TILES
+
+    merged = [merges(cols, c) for c in range(CHUNKS)]
 
     def fetch(src, dst, k):
         return pltpu.make_async_copy(src, dst, in_sem.at[k])
@@ -163,7 +172,7 @@
 
     def vertical(c):
         src = kv[c].at[(1 - row) * (blocks - 1)]
-        return copy(src, cbuf[c].at[2 * SLOTS], v_send.at[c], v_recv.at[c], other)
+        return copy(src, cbuf[c].at[cbuf[c].shape[0] - 1], v_send.at[c], v_recv.at[c], other)
 
     def local(k):
         return pltpu.make_async_copy(heard.at[k], heard_s.at[k], req_local.at[k])
@@ -193,8 +202,29 @@
 
     sides = ((0, has_left, col == 1, left), (1, has_right, col == cols - 2, right))
 
+    diagonal_step = 2 * gy - 1
+    gives = (gz + diagonal_step >= 0) & (gz + diagonal_step < LINE)
+    takes = (gz - diagonal_step >= 0) & (gz - diagonal_step < LINE)
+
+    def diagonal(c):
+        return copy(dsend[c], dbuf[c], d_send.at[c], d_recv.at[c], on_line(gz + diagonal_step))
+
     def send_sides(c):
         vertical(c).start()
+        if merged[c]:
+
+            @pl.when(gives)
+            def _():
+                low = 2 + blocks * (1 - gy)
+                entries = [
+                    jnp.where(gy == 0, heard_s[1, 0, i], heard_s[2, 0, i]) for i in range(4)
+                ]
+                rows = slot_rows(side_entries(entries, low, low + blocks), 2)
+                for j in range(2):
+                    dsend[c][j] = kv[c][rows[j]]
+                diagonal(c).start()
+
+            return
         for side, exists, edge, device in sides:
             low = 2 + blocks * (1 - side)
 
@@ -234,11 +264,28 @@
         for i in range(4):
             place, _ = line_place(heard_s[0, 0, 4 + i], gz * 2 + 1 - gy, distant)
             psend[c][i] = zbuf[c][place]
+        if merged[c]:
+            pl.when(takes)(lambda: diagonal(c).wait_recv())
+            entries = [heard_s[0, 0, i] for i in range(4)]
+            own_low, far_low = 2 + blocks * gy, 2 + blocks * (1 - gy)
+            own = side_entries(entries, own_low, own_low + blocks)
+            far = side_entries(entries, far_low, far_low + blocks)
+            across = side_entries(entries, 2, 2 + 2 * blocks)
+            for j in range(SLOTS):
+                here, row_at, far_at = jnp.bool_(False), jnp.int32(0), jnp.int32(0)
+                for o, f, a in zip(own, far, across):
+                    chosen = a[0] & (a[1] == j)
+                    here = here | (chosen & o[0])
+                    row_at = row_at + jnp.where(chosen & o[0], o[2], 0)
+                    far_at = far_at + jnp.where(chosen & f[0], f[1], 0)
+                psend[c][4 + j] = jnp.where(here, kv[c][row_at], dbuf[c][far_at])
         partner_copy(c).start()
 
     def wait_inputs(c):
         partner_copy(c).wait_recv()
         vertical(c).wait_recv()
+        if merged[c]:
+            return
         pl.when(has_left)(lambda: side_copy(c, 1, left).wait_recv())
         pl.when(has_right)(lambda: side_copy(c, 0, right).wait_recv())
         pl.when(col == cols - 1)(lambda: edge_copy(c, 1, left).wait_recv())
@@ -251,10 +298,16 @@
         jnp.where(a[0], a[1], jnp.where(b[0], SLOTS + b[1], 2 * SLOTS))
         for a, b in zip(lefts, rights)
     ]
+    acrosses = side_entries(entries, 2, 2 + 2 * blocks)
 
     def attend(c):
         for i in range(4):
-            kv[c][blocks + i] = cbuf[c][cycle_places[i]]
+            if merged[c]:
+                across, rank, _ = acrosses[i]
+                met = pbuf[c][4 + jnp.where(across, rank, 0)]
+                kv[c][blocks + i] = jnp.where(across, met, cbuf[c][0])
+            else:
+                kv[c][blocks + i] = cbuf[c][cycle_places[i]]
             place, crossing = line_place(dilated[i], member, distant)
             kv[c][blocks + 4 + i] = jnp.where(crossing, pbuf[c][i], zbuf[c][place])
         factor = HEAD_DIM**-0.5 * math.log2(math.e)
@@ -307,6 +360,9 @@
         pl.when((gz == 1) | (gz == 2))(lambda: line_copy(c, 0, 0, f_send.at[c]).wait_send())
         partner_copy(c).wait_send()
         vertical(c).wait_send()
+        if merged[c]:
+            pl.when(gives)(lambda: diagonal(c).wait_send())
+            continue
         pl.when(has_left)(lambda: side_copy(c, 0, left).wait_send())
         pl.when(has_right)(lambda: side_copy(c, 1, right).wait_send())
         pl.when(col == 1)(lambda: edge_copy(c, 0, left).wait_send())
@@ -322,8 +378,15 @@
     smem = pl.BlockSpec(memory_space=pltpu.SMEM)
     anywhere = pl.BlockSpec(memory_space=pl.ANY)
 
-    def buffers(slots):
-        return [vmem((slots, 2, block, width), jnp.bfloat16) for width in WIDTHS]
+    def buffers(slots, merged_slots=None):
+        slots_of = [
+            slots if merged_slots is None or not merges(cols, c) else merged_slots
+            for c in range(CHUNKS)
+        ]
+        return [
+            vmem((count, 2, block, width), jnp.bfloat16)
+            for count, width in zip(slots_of, WIDTHS)
+        ]
 
     dma = pltpu.SemaphoreType.DMA
     tokens = blocks * block
@@ -333,8 +396,9 @@
         in_specs=[smem] * 2 + [anywhere] * 5,
         out_specs=pl.BlockSpec(memory_space=vmem),
         scratch_shapes=[
-            *buffers(blocks + 8), *buffers(LINE * distant), *buffers(4),
-            *buffers(2 * SLOTS + 1), *buffers(4), *buffers(2 * SLOTS),
+            *buffers(blocks + 8), *buffers(LINE * distant), *buffers(4, 4 + SLOTS),
+            *buffers(2 * SLOTS + 1, 1), *buffers(4, 4 + SLOTS), *buffers(2 * SLOTS, 1),
+            *buffers(1, 2), *buffers(1, 2),
             vmem((tokens, features), jnp.bfloat16),
             *[
                 part
@@ -350,10 +414,10 @@
             dma((CHUNKS, 4)), dma((CHUNKS, LINE)), dma((CHUNKS,)),
             dma((CHUNKS,)), dma((CHUNKS,)),
             dma((CHUNKS, 2)), dma((CHUNKS, 2)), dma((CHUNKS, 2)), dma((CHUNKS, 2)),
-            dma((CHUNKS,)), dma((CHUNKS,)),
+            dma((CHUNKS,)), dma((CHUNKS,)), dma((CHUNKS,)), dma((CHUNKS,)),
         ],
         compiler_params=pltpu.CompilerParams(
-            collective_id=0, has_side_effects=True, vmem_limit_bytes=60 * 2**20
+            collective_id=0, has_side_effects=True, vmem_limit_bytes=57 * 2**20
         ),
         cost_estimate=pl.CostEstimate(
             flops=8 * tokens * tokens * features, bytes_accessed=10 * tokens * features,

time: 91.1 us -> 100 us (1.098); the launches traced: 91 us -> 98.8 us
  Pallas kernels: 88.3 us -> 96.2 us
    pallas_call x1, Pallas kernels: 88.3 us -> 96.2 us  [per_device(): pl.pallas_call(functools.partial(kernel, cols, blocks), out_shape=jax.Sha...]
where the time goes in v3:
time: 100 us; the launch traced here: 98.8 us
  Pallas kernels  96.2 us (96%)
  local copies, waits for them, and re-layouts  2.65 us (3%)
    pallas_call x1, Pallas kernels, per_device(): pl.pallas_call(functools.partial(kernel, cols, blocks), out_shape=jax.Sha...  96.2 us
    unnamed x1, local copies, waits for them, and re-layouts  2.65 us

profile of v3, /device:TPU:0, one launch (start us, length us, event | category | flops | bytes accessed | tf_op | source)
XLA Modules:
  0.0 98.8 jit_solution(8868382216003669896)
XLA Ops:
  0.0 96.2 %shard_map.73 = bf16[512,1536]{1,0:T(8,128)(2,1)} custom-call(s32[4]{0:T(128)} %bitcast.16, s32[4]{0:T(128)} %bitcast.17, bf16[512,1536]{1,0:T(8,128)(2,1)} %bitcast.11, bf16[8,64,1536]{2,1,0:T(8,128)(2,1)} %bitcast.12, s32[8,2,1536]{2,1,0:T(2,128)} %bitcast.14, bf16[8,64,1536]{2,1,0:T(8,128)(2,1)} %bitcast.13, s32[8,2,1536]{2,1,0:T(2,128)} %bitcast.15), custom_call_target="tpu_custom_call" | custom-call | flops 3221225472 | bytes 7864320 | tf_op jit(solution)/shard_map/pallas_call | solution.py:393
  96.2 2.7 %copy.10 = bf16[8,1,64,1536]{3,2,1,0:T(8,128)(2,1)} copy(bf16[8,1,64,1536]{3,2,1,0:T(8,128)(2,1)} %bitcast.10) | data formatting | bytes 3145728

commit v4 on v2

--- a/solution.py
+++ b/solution.py
@@ -12,11 +12,13 @@
 HEAD_DIM = 128
 DILATION_TILES = 8
 LINE = DILATION_TILES // 2
-CHUNK_HEADS = (1, 2, 2, 2, 2, 2, 1)
+CHUNK_HEADS = (2, 2, 2, 2, 2, 1, 1)
 CHUNKS = len(CHUNK_HEADS)
 STARTS = tuple(sum(CHUNK_HEADS[:c]) * HEAD_DIM for c in range(CHUNKS))
 WIDTHS = tuple(n * HEAD_DIM for n in CHUNK_HEADS)
-AHEAD = 3
+AHEAD = 4
+PARTNER_LAG = 1
+ATTEND_LAG = 3
 QUERY_TILE = 256
 SLOTS = 3
 MESH = pl.DeviceIdType.MESH
@@ -284,17 +286,17 @@
     for c in range(AHEAD):
         send_sides(c)
     queries.wait()
-    for c in range(CHUNKS):
-        forward(c)
-        send_partner(c)
-        if c + AHEAD < CHUNKS:
-            send_line(c + AHEAD)
-            send_sides(c + AHEAD)
-        if c:
-            wait_inputs(c - 1)
-            attend(c - 1)
-    wait_inputs(CHUNKS - 1)
-    attend(CHUNKS - 1)
+    for t in range(CHUNKS + ATTEND_LAG):
+        if t < CHUNKS:
+            forward(t)
+        if t + AHEAD < CHUNKS:
+            send_line(t + AHEAD)
+            send_sides(t + AHEAD)
+        if 0 <= t - PARTNER_LAG < CHUNKS:
+            send_partner(t - PARTNER_LAG)
+        if t >= ATTEND_LAG:
+            wait_inputs(t - ATTEND_LAG)
+            attend(t - ATTEND_LAG)
 
     ask(0, partner).wait_send()
     pl.when(has_left)(lambda: ask(2, left).wait_send())

time: 91.1 us -> 89.9 us (0.987); the launches traced: 91 us -> 88.8 us
  Pallas kernels: 88.3 us -> 86.1 us
    pallas_call x1, Pallas kernels: 88.3 us -> 86.1 us  [per_device(): pl.pallas_call(functools.partial(kernel, cols, blocks), out_shape=jax.Sha...]
where the time goes in v4:
time: 89.9 us; the launch traced here: 88.8 us
  Pallas kernels  86.1 us (96%)
  local copies, waits for them, and re-layouts  2.65 us (3%)
    pallas_call x1, Pallas kernels, per_device(): pl.pallas_call(functools.partial(kernel, cols, blocks), out_shape=jax.Sha...  86.1 us
    unnamed x1, local copies, waits for them, and re-layouts  2.65 us

profile of v4, /device:TPU:0, one launch (start us, length us, event | category | flops | bytes accessed | tf_op | source)
XLA Modules:
  0.0 88.8 jit_solution(374374449264158029)
XLA Ops:
  0.0 86.1 %shard_map.73 = bf16[512,1536]{1,0:T(8,128)(2,1)} custom-call(s32[4]{0:T(128)} %bitcast.16, s32[4]{0:T(128)} %bitcast.17, bf16[512,1536]{1,0:T(8,128)(2,1)} %bitcast.11, bf16[8,64,1536]{2,1,0:T(8,128)(2,1)} %bitcast.12, s32[8,2,1536]{2,1,0:T(2,128)} %bitcast.14, bf16[8,64,1536]{2,1,0:T(8,128)(2,1)} %bitcast.13, s32[8,2,1536]{2,1,0:T(2,128)} %bitcast.15), custom_call_target="tpu_custom_call" | custom-call | flops 3221225472 | bytes 7864320 | tf_op jit(solution)/shard_map/pallas_call | solution.py:332
  86.1 2.7 %copy.10 = bf16[8,1,64,1536]{3,2,1,0:T(8,128)(2,1)} copy(bf16[8,1,64,1536]{3,2,1,0:T(8,128)(2,1)} %bitcast.10) | data formatting | bytes 3145728

commit v5 on v4

--- a/solution.py
+++ b/solution.py
@@ -17,6 +17,7 @@
 STARTS = tuple(sum(CHUNK_HEADS[:c]) * HEAD_DIM for c in range(CHUNKS))
 WIDTHS = tuple(n * HEAD_DIM for n in CHUNK_HEADS)
 AHEAD = 4
+DIRECT_CHUNKS = 2
 PARTNER_LAG = 1
 ATTEND_LAG = 3
 QUERY_TILE = 256
@@ -47,6 +48,10 @@
     return place, lax.rem(hop, 2) == 1
 
 
+def merges(cols, c):
+    return cols == DILATION_TILES and c >= DIRECT_CHUNKS
+
+
 def kernel(cols, blocks, cycle, dilated, q_hbm, km_hbm, ke_hbm, vm_hbm, ve_hbm, out_ref, *scratch):
     kv = scratch[0:CHUNKS]
     zbuf = scratch[CHUNKS : 2 * CHUNKS]
@@ -54,12 +59,16 @@
     cbuf = scratch[3 * CHUNKS : 4 * CHUNKS]
     psend = scratch[4 * CHUNKS : 5 * CHUNKS]
     csend = scratch[5 * CHUNKS : 6 * CHUNKS]
+    dsend = scratch[6 * CHUNKS : 7 * CHUNKS]
+    dbuf = scratch[7 * CHUNKS : 8 * CHUNKS]
     (q_ref, km_ref, ke_ref, vm_ref, ve_ref, in_sem, asked, heard, heard_s, req_send, req_recv, req_local, z_send, z_recv, f_send, p_send, p_recv,
-     c_send, c_recv, e_send, e_recv, v_send, v_recv) = scratch[6 * CHUNKS :]
+     c_send, c_recv, e_send, e_recv, v_send, v_recv, d_send, d_recv) = scratch[8 * CHUNKS :]
     block = kv[0].shape[-2]
     groups = ke_ref.shape[1]
     distant = blocks // 4
     spacing = cols // DILATION_TILES
+
+    merged = [merges(cols, c) for c in range(CHUNKS)]
 
     def fetch(src, dst, k):
         return pltpu.make_async_copy(src, dst, in_sem.at[k])
@@ -165,7 +174,7 @@
 
     def vertical(c):
         src = kv[c].at[(1 - row) * (blocks - 1)]
-        return copy(src, cbuf[c].at[2 * SLOTS], v_send.at[c], v_recv.at[c], other)
+        return copy(src, cbuf[c].at[cbuf[c].shape[0] - 1], v_send.at[c], v_recv.at[c], other)
 
     def local(k):
         return pltpu.make_async_copy(heard.at[k], heard_s.at[k], req_local.at[k])
@@ -195,8 +204,29 @@
 
     sides = ((0, has_left, col == 1, left), (1, has_right, col == cols - 2, right))
 
+    diagonal_step = 2 * gy - 1
+    gives = (gz + diagonal_step >= 0) & (gz + diagonal_step < LINE)
+    takes = (gz - diagonal_step >= 0) & (gz - diagonal_step < LINE)
+
+    def diagonal(c):
+        return copy(dsend[c], dbuf[c], d_send.at[c], d_recv.at[c], on_line(gz + diagonal_step))
+
     def send_sides(c):
         vertical(c).start()
+        if merged[c]:
+
+            @pl.when(gives)
+            def _():
+                low = 2 + blocks * (1 - gy)
+                entries = [
+                    jnp.where(gy == 0, heard_s[1, 0, i], heard_s[2, 0, i]) for i in range(4)
+                ]
+                rows = slot_rows(side_entries(entries, low, low + blocks), 2)
+                for j in range(2):
+                    dsend[c][j] = kv[c][rows[j]]
+                diagonal(c).start()
+
+            return
         for side, exists, edge, device in sides:
             low = 2 + blocks * (1 - side)
 
@@ -223,6 +253,28 @@
         def _():
             line_copy(c, 0, 2, z_send.at[c, 0]).wait_recv()
             line_copy(c, 0, 3, f_send.at[c]).start()
+
+    def merged_copy(c):
+        return copy(
+            csend[c], cbuf[c].at[pl.ds(0, SLOTS)], c_send.at[c, 0], c_recv.at[c, 0], partner
+        )
+
+    def send_merged(c):
+        pl.when(takes)(lambda: diagonal(c).wait_recv())
+        entries = [heard_s[0, 0, i] for i in range(4)]
+        own_low, far_low = 2 + blocks * gy, 2 + blocks * (1 - gy)
+        own = side_entries(entries, own_low, own_low + blocks)
+        far = side_entries(entries, far_low, far_low + blocks)
+        across = side_entries(entries, 2, 2 + 2 * blocks)
+        for j in range(SLOTS):
+            here, row_at, far_at = jnp.bool_(False), jnp.int32(0), jnp.int32(0)
+            for o, f, a in zip(own, far, across):
+                chosen = a[0] & (a[1] == j)
+                here = here | (chosen & o[0])
+                row_at = row_at + jnp.where(chosen & o[0], o[2], 0)
+                far_at = far_at + jnp.where(chosen & f[0], f[1], 0)
+            csend[c][j] = jnp.where(here, kv[c][row_at], dbuf[c][far_at])
+        merged_copy(c).start()
 
     def partner_copy(c):
         return copy(psend[c], pbuf[c], p_send.at[c], p_recv.at[c], partner)
@@ -241,6 +293,9 @@
     def wait_inputs(c):
         partner_copy(c).wait_recv()
         vertical(c).wait_recv()
+        if merged[c]:
+            merged_copy(c).wait_recv()
+            return
         pl.when(has_left)(lambda: side_copy(c, 1, left).wait_recv())
         pl.when(has_right)(lambda: side_copy(c, 0, right).wait_recv())
         pl.when(col == cols - 1)(lambda: edge_copy(c, 1, left).wait_recv())
@@ -253,10 +308,13 @@
         jnp.where(a[0], a[1], jnp.where(b[0], SLOTS + b[1], 2 * SLOTS))
         for a, b in zip(lefts, rights)
     ]
+    merged_places = [
+        jnp.where(hit, rank, SLOTS) for hit, rank, _ in side_entries(entries, 2, 2 + 2 * blocks)
+    ]
 
     def attend(c):
         for i in range(4):
-            kv[c][blocks + i] = cbuf[c][cycle_places[i]]
+            kv[c][blocks + i] = cbuf[c][(merged_places if merged[c] else cycle_places)[i]]
             place, crossing = line_place(dilated[i], member, distant)
             kv[c][blocks + 4 + i] = jnp.where(crossing, pbuf[c][i], zbuf[c][place])
         factor = HEAD_DIM**-0.5 * math.log2(math.e)
@@ -289,6 +347,8 @@
     for t in range(CHUNKS + ATTEND_LAG):
         if t < CHUNKS:
             forward(t)
+            if merged[t]:
+                send_merged(t)
         if t + AHEAD < CHUNKS:
             send_line(t + AHEAD)
             send_sides(t + AHEAD)
@@ -309,6 +369,10 @@
         pl.when((gz == 1) | (gz == 2))(lambda: line_copy(c, 0, 0, f_send.at[c]).wait_send())
         partner_copy(c).wait_send()
         vertical(c).wait_send()
+        if merged[c]:
+            pl.when(gives)(lambda: diagonal(c).wait_send())
+            merged_copy(c).wait_send()
+            continue
         pl.when(has_left)(lambda: side_copy(c, 0, left).wait_send())
         pl.when(has_right)(lambda: side_copy(c, 1, right).wait_send())
         pl.when(col == 1)(lambda: edge_copy(c, 0, left).wait_send())
@@ -324,8 +388,15 @@
     smem = pl.BlockSpec(memory_space=pltpu.SMEM)
     anywhere = pl.BlockSpec(memory_space=pl.ANY)
 
-    def buffers(slots):
-        return [vmem((slots, 2, block, width), jnp.bfloat16) for width in WIDTHS]
+    def buffers(slots, merged_slots=None):
+        slots_of = [
+            slots if merged_slots is None or not merges(cols, c) else merged_slots
+            for c in range(CHUNKS)
+        ]
+        return [
+            vmem((count, 2, block, width), jnp.bfloat16)
+            for count, width in zip(slots_of, WIDTHS)
+        ]
 
     dma = pltpu.SemaphoreType.DMA
     tokens = blocks * block
@@ -336,7 +407,8 @@
         out_specs=pl.BlockSpec(memory_space=vmem),
         scratch_shapes=[
             *buffers(blocks + 8), *buffers(LINE * distant), *buffers(4),
-            *buffers(2 * SLOTS + 1), *buffers(4), *buffers(2 * SLOTS),
+            *buffers(2 * SLOTS + 1, SLOTS + 1), *buffers(4), *buffers(2 * SLOTS, SLOTS),
+            *buffers(1, 2), *buffers(1, 2),
             vmem((tokens, features), jnp.bfloat16),
             *[
                 part
@@ -352,7 +424,7 @@
             dma((CHUNKS, 4)), dma((CHUNKS, LINE)), dma((CHUNKS,)),
             dma((CHUNKS,)), dma((CHUNKS,)),
             dma((CHUNKS, 2)), dma((CHUNKS, 2)), dma((CHUNKS, 2)), dma((CHUNKS, 2)),
-            dma((CHUNKS,)), dma((CHUNKS,)),
+            dma((CHUNKS,)), dma((CHUNKS,)), dma((CHUNKS,)), dma((CHUNKS,)),
         ],
         compiler_params=pltpu.CompilerParams(
             collective_id=0, has_side_effects=True, vmem_limit_bytes=60 * 2**20

time: 89.9 us -> 103 us (1.15)
  the two profiles are of different devices: /device:TPU:0 before, /device:TPU:18 now
where the time goes in v5:
time: 103 us
  Pallas kernels  100 us (97%)
  local copies, waits for them, and re-layouts  2.65 us (3%)
    pallas_call x1, Pallas kernels, per_device(): pl.pallas_call(functools.partial(kernel, cols, blocks), out_shape=jax.Sha...  100 us
    unnamed x1, local copies, waits for them, and re-layouts  2.65 us

profile of v5, /device:TPU:18, one launch (start us, length us, event | category | flops | bytes accessed | tf_op | source)
XLA Modules:
  0.0 102.9 jit_solution(10332594108315683701)
XLA Ops:
  0.0 100.2 %shard_map.73 = bf16[512,1536]{1,0:T(8,128)(2,1)} custom-call(s32[4]{0:T(128)} %bitcast.16, s32[4]{0:T(128)} %bitcast.17, bf16[512,1536]{1,0:T(8,128)(2,1)} %bitcast.11, bf16[8,64,1536]{2,1,0:T(8,128)(2,1)} %bitcast.12, s32[8,2,1536]{2,1,0:T(2,128)} %bitcast.14, bf16[8,64,1536]{2,1,0:T(8,128)(2,1)} %bitcast.13, s32[8,2,1536]{2,1,0:T(2,128)} %bitcast.15), custom_call_target="tpu_custom_call" | custom-call | flops 3221225472 | bytes 7864320 | tf_op jit(solution)/shard_map/pallas_call | solution.py:403
  100.3 2.7 %copy.10 = bf16[8,1,64,1536]{3,2,1,0:T(8,128)(2,1)} copy(bf16[8,1,64,1536]{3,2,1,0:T(8,128)(2,1)} %bitcast.10) | data formatting | bytes 3145728

commit v6 on v4

--- a/solution.py
+++ b/solution.py
@@ -12,11 +12,11 @@
 HEAD_DIM = 128
 DILATION_TILES = 8
 LINE = DILATION_TILES // 2
-CHUNK_HEADS = (2, 2, 2, 2, 2, 1, 1)
+CHUNK_HEADS = (1,) * HEADS
 CHUNKS = len(CHUNK_HEADS)
 STARTS = tuple(sum(CHUNK_HEADS[:c]) * HEAD_DIM for c in range(CHUNKS))
 WIDTHS = tuple(n * HEAD_DIM for n in CHUNK_HEADS)
-AHEAD = 4
+AHEAD = 3
 PARTNER_LAG = 1
 ATTEND_LAG = 3
 QUERY_TILE = 256
@@ -144,7 +144,7 @@
         part = zbuf[c].at[pl.ds(source * distant, distant)]
         return copy(part, part, sem, z_recv.at[c, source], on_line(z))
 
-    steps = (1, -1, 2, -2)
+    steps = (2, -2, 1, -1)
 
     def reaches(step):
         return (gz + step >= 0) & (gz + step < LINE)

time: 89.9 us -> 86.8 us (0.966)
  Pallas kernels: 86.1 us -> 82.9 us
    pallas_call x1, Pallas kernels: 86.1 us -> 82.9 us  [per_device(): pl.pallas_call(functools.partial(kernel, cols, blocks), out_shape=jax.Sha...]
where the time goes in v6:
time: 86.8 us; the launch traced here: 85.6 us
  Pallas kernels  82.9 us (96%)
  local copies, waits for them, and re-layouts  2.65 us (3%)
    pallas_call x1, Pallas kernels, per_device(): pl.pallas_call(functools.partial(kernel, cols, blocks), out_shape=jax.Sha...  82.9 us
    unnamed x1, local copies, waits for them, and re-layouts  2.65 us

profile of v6, /device:TPU:0, one launch (start us, length us, event | category | flops | bytes accessed | tf_op | source)
XLA Modules:
  0.0 85.6 jit_solution(9368148410187908496)
XLA Ops:
  0.0 82.9 %shard_map.73 = bf16[512,1536]{1,0:T(8,128)(2,1)} custom-call(s32[4]{0:T(128)} %bitcast.16, s32[4]{0:T(128)} %bitcast.17, bf16[512,1536]{1,0:T(8,128)(2,1)} %bitcast.11, bf16[8,64,1536]{2,1,0:T(8,128)(2,1)} %bitcast.12, s32[8,2,1536]{2,1,0:T(2,128)} %bitcast.14, bf16[8,64,1536]{2,1,0:T(8,128)(2,1)} %bitcast.13, s32[8,2,1536]{2,1,0:T(2,128)} %bitcast.15), custom_call_target="tpu_custom_call" | custom-call | flops 3221225472 | bytes 7864320 | tf_op jit(solution)/shard_map/pallas_call | solution.py:332
  82.9 2.7 %copy.10 = bf16[8,1,64,1536]{3,2,1,0:T(8,128)(2,1)} copy(bf16[8,1,64,1536]{3,2,1,0:T(8,128)(2,1)} %bitcast.10) | data formatting | bytes 3145728

commit v7 on v6

--- a/solution.py
+++ b/solution.py
@@ -17,6 +17,7 @@
 STARTS = tuple(sum(CHUNK_HEADS[:c]) * HEAD_DIM for c in range(CHUNKS))
 WIDTHS = tuple(n * HEAD_DIM for n in CHUNK_HEADS)
 AHEAD = 3
+SIDES_AHEAD = 6
 PARTNER_LAG = 1
 ATTEND_LAG = 3
 QUERY_TILE = 256
@@ -47,14 +48,14 @@
     return place, lax.rem(hop, 2) == 1
 
 
-def kernel(cols, blocks, cycle, dilated, q_hbm, km_hbm, ke_hbm, vm_hbm, ve_hbm, out_ref, *scratch):
+def kernel(cols, blocks, cycle, dilated, q_hbm, km_hbm, ke_hbm, vm_hbm, ve_hbm, out_hbm, *scratch):
     kv = scratch[0:CHUNKS]
     zbuf = scratch[CHUNKS : 2 * CHUNKS]
     pbuf = scratch[2 * CHUNKS : 3 * CHUNKS]
     cbuf = scratch[3 * CHUNKS : 4 * CHUNKS]
     psend = scratch[4 * CHUNKS : 5 * CHUNKS]
     csend = scratch[5 * CHUNKS : 6 * CHUNKS]
-    (q_ref, km_ref, ke_ref, vm_ref, ve_ref, in_sem, asked, heard, heard_s, req_send, req_recv, req_local, z_send, z_recv, f_send, p_send, p_recv,
+    (out_ref, out_sem, q_ref, km_ref, ke_ref, vm_ref, ve_ref, in_sem, asked, heard, heard_s, req_send, req_recv, req_local, z_send, z_recv, f_send, p_send, p_recv,
      c_send, c_recv, e_send, e_recv, v_send, v_recv) = scratch[6 * CHUNKS :]
     block = kv[0].shape[-2]
     groups = ke_ref.shape[1]
@@ -253,6 +254,10 @@
         jnp.where(a[0], a[1], jnp.where(b[0], SLOTS + b[1], 2 * SLOTS))
         for a, b in zip(lefts, rights)
     ]
+
+    def deliver(c):
+        lanes = pl.ds(STARTS[c], WIDTHS[c])
+        return pltpu.make_async_copy(out_ref.at[:, lanes], out_hbm.at[:, lanes], out_sem.at[c])
 
     def attend(c):
         for i in range(4):
@@ -282,8 +287,9 @@
             return carry
 
         lax.fori_loop(0, q_ref.shape[0] // QUERY_TILE, tile, 0)
-
-    for c in range(AHEAD):
+        deliver(c).start()
+
+    for c in range(SIDES_AHEAD):
         send_sides(c)
     queries.wait()
     for t in range(CHUNKS + ATTEND_LAG):
@@ -291,7 +297,8 @@
             forward(t)
         if t + AHEAD < CHUNKS:
             send_line(t + AHEAD)
-            send_sides(t + AHEAD)
+        if t + SIDES_AHEAD < CHUNKS:
+            send_sides(t + SIDES_AHEAD)
         if 0 <= t - PARTNER_LAG < CHUNKS:
             send_partner(t - PARTNER_LAG)
         if t >= ATTEND_LAG:
@@ -307,6 +314,7 @@
                 lambda c=c, k=k, step=step: line_copy(c, gz, gz, z_send.at[c, k]).wait_send()
             )
         pl.when((gz == 1) | (gz == 2))(lambda: line_copy(c, 0, 0, f_send.at[c]).wait_send())
+        deliver(c).wait()
         partner_copy(c).wait_send()
         vertical(c).wait_send()
         pl.when(has_left)(lambda: side_copy(c, 0, left).wait_send())
@@ -333,10 +341,11 @@
         functools.partial(kernel, cols, blocks),
         out_shape=jax.ShapeDtypeStruct((tokens, features), jnp.bfloat16),
         in_specs=[smem] * 2 + [anywhere] * 5,
-        out_specs=pl.BlockSpec(memory_space=vmem),
+        out_specs=anywhere,
         scratch_shapes=[
             *buffers(blocks + 8), *buffers(LINE * distant), *buffers(4),
             *buffers(2 * SLOTS + 1), *buffers(4), *buffers(2 * SLOTS),
+            vmem((tokens, features), jnp.bfloat16), dma((CHUNKS,)),
             vmem((tokens, features), jnp.bfloat16),
             *[
                 part

time: 86.8 us -> 84.7 us (0.976); the launches traced: 85.6 us -> 84.6 us
  Pallas kernels: 82.9 us -> 81.9 us
    pallas_call x1, Pallas kernels: 82.9 us -> 81.9 us  [per_device(): pl.pallas_call(functools.partial(kernel, cols, blocks), out_shape=jax.Sha...]
where the time goes in v7:
time: 84.7 us; the launch traced here: 84.6 us
  Pallas kernels  81.9 us (97%)
  local copies, waits for them, and re-layouts  2.65 us (3%)
    pallas_call x1, Pallas kernels, per_device(): pl.pallas_call(functools.partial(kernel, cols, blocks), out_shape=jax.Sha...  81.9 us
    unnamed x1, local copies, waits for them, and re-layouts  2.65 us

profile of v7, /device:TPU:0, one launch (start us, length us, event | category | flops | bytes accessed | tf_op | source)
XLA Modules:
  0.0 84.6 jit_solution(10743678943761934042)
XLA Ops:
  0.0 81.9 %shard_map.73 = bf16[512,1536]{1,0:T(8,128)(2,1)} custom-call(s32[4]{0:T(128)} %bitcast.16, s32[4]{0:T(128)} %bitcast.17, bf16[512,1536]{1,0:T(8,128)(2,1)} %bitcast.11, bf16[8,64,1536]{2,1,0:T(8,128)(2,1)} %bitcast.12, s32[8,2,1536]{2,1,0:T(2,128)} %bitcast.14, bf16[8,64,1536]{2,1,0:T(8,128)(2,1)} %bitcast.13, s32[8,2,1536]{2,1,0:T(2,128)} %bitcast.15), custom_call_target="tpu_custom_call" | custom-call | flops 3221225472 | bytes 7864320 | tf_op jit(solution)/shard_map/pallas_call | solution.py:340
  81.9 2.7 %copy.10 = bf16[8,1,64,1536]{3,2,1,0:T(8,128)(2,1)} copy(bf16[8,1,64,1536]{3,2,1,0:T(8,128)(2,1)} %bitcast.10) | data formatting | bytes 3145728

commit v8 on v7

--- a/solution.py
+++ b/solution.py
@@ -17,7 +17,7 @@
 STARTS = tuple(sum(CHUNK_HEADS[:c]) * HEAD_DIM for c in range(CHUNKS))
 WIDTHS = tuple(n * HEAD_DIM for n in CHUNK_HEADS)
 AHEAD = 3
-SIDES_AHEAD = 6
+SIDES_AHEAD = 9
 PARTNER_LAG = 1
 ATTEND_LAG = 3
 QUERY_TILE = 256

time: 84.7 us -> 88.1 us (1.040)
  Pallas kernels: 81.9 us -> 85.3 us
    pallas_call x1, Pallas kernels: 81.9 us -> 85.3 us  [per_device(): pl.pallas_call(functools.partial(kernel, cols, blocks), out_shape=jax.Sha...]
where the time goes in v8:
time: 88.1 us; the launch traced here: 87.9 us
  Pallas kernels  85.3 us (97%)
  local copies, waits for them, and re-layouts  2.65 us (3%)
    pallas_call x1, Pallas kernels, per_device(): pl.pallas_call(functools.partial(kernel, cols, blocks), out_shape=jax.Sha...  85.3 us
    unnamed x1, local copies, waits for them, and re-layouts  2.65 us

profile of v8, /device:TPU:0, one launch (start us, length us, event | category | flops | bytes accessed | tf_op | source)
XLA Modules:
  0.0 87.9 jit_solution(3806348700760208024)
XLA Ops:
  0.0 85.3 %shard_map.73 = bf16[512,1536]{1,0:T(8,128)(2,1)} custom-call(s32[4]{0:T(128)} %bitcast.16, s32[4]{0:T(128)} %bitcast.17, bf16[512,1536]{1,0:T(8,128)(2,1)} %bitcast.11, bf16[8,64,1536]{2,1,0:T(8,128)(2,1)} %bitcast.12, s32[8,2,1536]{2,1,0:T(2,128)} %bitcast.14, bf16[8,64,1536]{2,1,0:T(8,128)(2,1)} %bitcast.13, s32[8,2,1536]{2,1,0:T(2,128)} %bitcast.15), custom_call_target="tpu_custom_call" | custom-call | flops 3221225472 | bytes 7864320 | tf_op jit(solution)/shard_map/pallas_call | solution.py:340
  85.3 2.7 %copy.10 = bf16[8,1,64,1536]{3,2,1,0:T(8,128)(2,1)} copy(bf16[8,1,64,1536]{3,2,1,0:T(8,128)(2,1)} %bitcast.10) | data formatting | bytes 3145728
